TPU v7x, 32 devices: a whole 2x2x4 slice. The times are simulated.
32 devices in a mesh: pairs: 8 (over y, x, core), aux: 4 (over z).
Axes of the slice: x: 2, y: 2, z: 4, core: 2. Of those that a mesh axis runs over, the one named last changes fastest.
Arguments:
- pair_orbits: int32 [512, 2], P('pairs'), may hold values from 0 to 255
- pno_count: int32 [512], P('pairs'), may hold values from 64 to 128
- partner: int32 [512, 12], P('pairs', 'aux'), may hold values from -1 to 511, as said below
- couple_orbit: int32 [512, 12], P('pairs', 'aux'), may hold values from 0 to 255
- couple_side: int32 [512, 12], P('pairs', 'aux'), may hold values from 0 to 1
- occ_fock: float32 [256, 256], replicated, may hold values from -2 to 1, as said below
- fit_left: bfloat16 [512, 128, 2048], P('pairs', None, 'aux'), may hold values from -0.8984375 to 0.8984375
- fit_right: bfloat16 [512, 128, 2048], P('pairs', None, 'aux'), may hold values from -0.8984375 to 0.8984375
- pno_coef: bfloat16 [512, 256, 128], P('pairs'), may hold values from -0.375 to 0.375
- virt_fock: bfloat16 [512, 128, 128], P('pairs'), may hold values from -0.25 to 3, as said below
- amps_in: float32 [512, 128, 128], P('pairs', 'aux'), may hold values from -1.8 to 1.8
Outputs:
- amps_out: float32 [512, 128, 128], P('pairs', 'aux')
Inputs may be any that keep to these rules, and one draw needn't show every extreme that they name: partner[p, c] is -1 (no coupling) or a pair held by another index of pairs; couplings are mutual: if slot c of p names q then slot c of q names p. In each slot, the pairs of one index of pairs name pairs of one other index at most 2 times, and 2 is reached in every slot. `occ_fock`: symmetric; its diagonal lies between -2 and -0.3. `virt_fock`: symmetric in its last two dimensions; its diagonal lies between 0.5 and 3.
All inputs are finite; a program needn't handle non-finite values.
Results may differ from a plain program's by a relative error of at most 0.0019.
Values may be sent and summed in bfloat16 or wider, within the bound.
No kernel may reach another device: no remote copies, remote signals or barrier semaphores. Data moves between devices by JAX's collectives and lax.ppermute only.
A program may use at most 192 MiB of HBM per device.

v0:
```python
import jax
import jax.numpy as jnp
from jax import lax
from jax.sharding import PartitionSpec as P

MOST = 2
ITERS = 2


precise = lax.Precision.HIGHEST


def slot_layout(targets, pair_dev, dev_count):
    is_valid = targets >= 0
    owner_dev = jnp.where(is_valid, targets // pair_dev, -1)
    local_ids = jnp.arange(pair_dev, dtype=jnp.int32)
    same_owner = (owner_dev[:, None] == owner_dev[None, :]) & is_valid[:, None] & is_valid[None, :]
    send_rank = jnp.sum(
        (same_owner & (local_ids[None, :] < local_ids[:, None])).astype(jnp.int32), axis=1
    )
    read_rank = jnp.sum(
        (same_owner & (targets[None, :] < targets[:, None])).astype(jnp.int32), axis=1
    )
    send_place = jnp.where(is_valid, owner_dev * MOST + send_rank, dev_count * MOST)
    read_place = jnp.where(is_valid, owner_dev * MOST + read_rank, 0)
    return (is_valid, send_place, read_place)


def pack_slots(values, send_place, dev_count):
    blank_buffer = jnp.zeros((dev_count * MOST,) + values.shape[1:], values.dtype)
    filled = blank_buffer.at[send_place].set(values, mode="drop")
    return filled.reshape((dev_count, MOST) + values.shape[1:])


def read_slots(received, read_place):
    flattened = received.reshape((-1,) + received.shape[2:])
    return jnp.take(flattened, read_place, axis=0)


def coupled_term(projector, far_amps, slot_weight):
    mixed_amp = jnp.einsum(
        "pab,pbc->pac", projector, far_amps, preferred_element_type=jnp.float32
    ).astype(jnp.bfloat16)
    image = jnp.einsum("pac,pdc->pad", mixed_amp, projector, preferred_element_type=jnp.float32)
    return slot_weight[:, None, None] * image


def per_device(
    pair_orbits,
    pno_count,
    partner,
    couple_orbit,
    couple_side,
    occ_fock,
    fit_left,
    fit_right,
    pno_coef,
    virt_fock,
    amps_in,
):
    pair_dev = pno_count.shape[0]
    pno_width = virt_fock.shape[1]
    row_count = amps_in.shape[1]
    slot_count = partner.shape[1]
    dev_count = lax.axis_size("pairs")
    row_start = lax.axis_index("aux") * row_count
    orbit_ids = jnp.arange(pno_width, dtype=jnp.int32)
    keep_vec = (orbit_ids[None, :] < pno_count[:, None]).astype(jnp.float32)
    keep_rows = lax.dynamic_slice_in_dim(keep_vec, row_start, row_count, 1)
    keep_mask = keep_rows[:, :, None] * keep_vec[:, None, :]
    fock_diag = jnp.diagonal(virt_fock, axis1=1, axis2=2).astype(jnp.float32)
    diag_rows = lax.dynamic_slice_in_dim(fock_diag, row_start, row_count, 1)
    occ_ids = jnp.arange(occ_fock.shape[0], dtype=jnp.int32)
    occ_diag = jnp.diagonal(occ_fock)
    occ_energy = jnp.sum(
        jnp.where(pair_orbits[:, :, None] == occ_ids[None, None, :], occ_diag[None, None, :], 0.0),
        axis=(1, 2),
    )
    denominator = diag_rows[:, :, None] + fock_diag[:, None, :] - occ_energy[:, None, None]
    free_orbit = jnp.where(couple_side == 0, pair_orbits[:, 0:1], pair_orbits[:, 1:2])
    onehot = (couple_orbit.reshape(-1)[:, None] == occ_ids[None, :]).astype(jnp.float32)
    fock_rows = jnp.dot(onehot, occ_fock, precision=precise)
    weight = -jnp.sum(
        jnp.where(free_orbit.reshape(-1)[:, None] == occ_ids[None, :], fock_rows, 0.0), axis=1
    )
    weight = weight.reshape(pair_dev, slot_count)
    layouts = [
        slot_layout(partner[:, slot_id], pair_dev, dev_count) for slot_id in range(slot_count)
    ]
    slot_weights = [
        jnp.where(layouts[slot_id][0], weight[:, slot_id], 0.0) for slot_id in range(slot_count)
    ]
    partial_k = jnp.einsum("pax,pbx->pab", fit_left, fit_right, preferred_element_type=jnp.float32)
    integral_rows = lax.psum_scatter(partial_k, "aux", scatter_dimension=1, tiled=True)
    amps_rows = amps_in * keep_mask
    full_half = lax.all_gather(amps_rows.astype(jnp.bfloat16), "aux", axis=1, tiled=True)
    row_fock = lax.dynamic_slice_in_dim(virt_fock, row_start, row_count, 1)
    projectors = []
    for update in range(ITERS):
        if update == 0:
            arrivals = []
            for slot_id in range(slot_count):
                coef_buffer = pack_slots(pno_coef, layouts[slot_id][1], dev_count)
                amps_buffer = pack_slots(full_half, layouts[slot_id][1], dev_count)
                arrivals.append(
                    (
                        lax.all_to_all(
                            coef_buffer, "pairs", split_axis=0, concat_axis=0, tiled=True
                        ),
                        lax.all_to_all(
                            amps_buffer, "pairs", split_axis=0, concat_axis=0, tiled=True
                        ),
                    )
                )
            coupling = jnp.zeros((pair_dev, pno_width, pno_width), jnp.float32)
            for slot_id in range(slot_count):
                far_coef = read_slots(arrivals[slot_id][0], layouts[slot_id][2])
                far_amps = read_slots(arrivals[slot_id][1], layouts[slot_id][2])
                projector = jnp.einsum(
                    "pvn,pvm->pnm", pno_coef, far_coef, preferred_element_type=jnp.float32
                ).astype(jnp.bfloat16)
                projectors.append(projector)
                coupling = coupling + coupled_term(projector, far_amps, slot_weights[slot_id])
        else:
            arrivals = []
            for slot_id in range(slot_count):
                amps_buffer = pack_slots(full_half, layouts[slot_id][1], dev_count)
                arrivals.append(
                    lax.all_to_all(amps_buffer, "pairs", split_axis=0, concat_axis=0, tiled=True)
                )
            coupling = jnp.zeros((pair_dev, pno_width, pno_width), jnp.float32)
            for slot_id in range(slot_count):
                far_amps = read_slots(arrivals[slot_id], layouts[slot_id][2])
                coupling = coupling + coupled_term(
                    projectors[slot_id], far_amps, slot_weights[slot_id]
                )
        coupling_share = lax.psum_scatter(coupling, "aux", scatter_dimension=1, tiled=True)
        rows_half = lax.dynamic_slice_in_dim(full_half, row_start, row_count, 1)
        left_term = jnp.einsum(
            "pab,pbc->pac", row_fock, full_half, preferred_element_type=jnp.float32
        )
        right_term = jnp.einsum(
            "pab,pbc->pac", rows_half, virt_fock, preferred_element_type=jnp.float32
        )
        residual = (
            integral_rows
            + left_term
            + right_term
            - occ_energy[:, None, None] * amps_rows
            + coupling_share
        )
        amps_rows = (amps_rows - residual / denominator) * keep_mask
        if update + 1 < ITERS:
            full_half = lax.all_gather(amps_rows.astype(jnp.bfloat16), "aux", axis=1, tiled=True)
    return amps_rows


def solution(mesh):
    return jax.shard_map(
        per_device,
        mesh=mesh,
        in_specs=(
            P("pairs", None),
            P("pairs"),
            P("pairs", "aux"),
            P("pairs", "aux"),
            P("pairs", "aux"),
            P(),
            P("pairs", None, "aux"),
            P("pairs", None, "aux"),
            P("pairs", None, None),
            P("pairs", None, None),
            P("pairs", "aux", None),
        ),
        out_specs=P("pairs", "aux", None),
        check_vma=False,
    )
```

profile of v0, /device:TPU:0, one launch (start us, length us, event | category | flops | bytes accessed | tf_op | source)
XLA Modules:
  0.0 476.6 jit_solution(2484180346776174006)
XLA Ops:
  7.4 2.4 fusion.98
  9.9 10.1 %fusion.144 = f32[64,128,128]{2,1,0:T(8,128)} fusion(bf16[64,128,512]{2,1,0:T(8,128)(2,1)} %param.21, bf16[64,128,512]{2,1,0:T(8,128)(2,1)} %param.22), kind=kOutput, calls=%fused_computation.206 | convolution fusion | flops 1073741824 | bytes 20971520 | tf_op jit(solution)/shard_map/pax,pbx->pab/dot_general | solution.py:93
  22.3 1.2 broadcast.265.clone
  23.4 12.7 %scatter_fusion.2 = bf16[16,256,128]{2,1,0:T(8,128)(2,1)} fusion(bf16[16,256,128]{2,1,0:T(8,128)(2,1)} %broadcast.265.clone, s32[64]{0:T(128)S(1)} %get-tuple-element.48, bf16[64,256,128]{2,1,0:T(8,128)(2,1)} %param.23), kind=kCustom, calls=%fused_computation.13 | custom fusion | bytes 12583168 | tf_op jit(solution)/shard_map/scatter | solution.py:31
  36.1 4.7 all-to-all-start.2
  40.8 1.2 broadcast.265.clone.1
  42.0 12.5 %scatter_fusion = bf16[16,256,128]{2,1,0:T(8,128)(2,1)} fusion(bf16[16,256,128]{2,1,0:T(8,128)(2,1)} %broadcast.265.clone.1, s32[64]{0:T(128)S(1)} %get-tuple-element.47, bf16[64,256,128]{2,1,0:T(8,128)(2,1)} %param.23), kind=kCustom, calls=%fused_computation.11 | custom fusion | bytes 12583168 | tf_op jit(solution)/shard_map/scatter | solution.py:31
  54.4 1.8 all-to-all-done.2
  56.2 3.6 all-to-all-start
  60.3 1.2 broadcast.265.clone.2
  61.5 12.6 %scatter_fusion.4 = bf16[16,256,128]{2,1,0:T(8,128)(2,1)} fusion(bf16[16,256,128]{2,1,0:T(8,128)(2,1)} %broadcast.265.clone.2, s32[64]{0:T(128)S(1)} %get-tuple-element.31, bf16[64,256,128]{2,1,0:T(8,128)(2,1)} %param.23), kind=kCustom, calls=%fused_computation.15 | custom fusion | bytes 12583168 | tf_op jit(solution)/shard_map/scatter | solution.py:31
  74.1 1.0 all-to-all-done
  75.1 3.6 all-to-all-start.4
  79.2 1.2 compare_and_fusion
  80.7 3.0 gather_fusion.4
  83.7 3.1 gather_fusion.2
  86.8 7.2 %all-to-all-done.4 = bf16[8,2,256,128]{3,2,1,0:T(8,128)(2,1)S(1)} async-done(((bf16[8,2,256,128]{3,2,1,0:T(8,128)(2,1)}), bf16[8,2,256,128]{3,2,1,0:T(8,128)(2,1)S(1)}, u32[]{:S(2)}, u32[]{:S(2)}) %all-to-all-start.4) | async-done | bytes 1048608 | tf_op jit(solution)/shard_map/all_to_all | solution.py:107
  94.0 3.1 gather_fusion.6
  97.1 0.9 broadcast.269.clone
  98.0 11.2 %scatter_fusion.3 = bf16[16,128,128]{2,1,0:T(8,128)(2,1)} fusion(bf16[16,128,128]{2,1,0:T(8,128)(2,1)} %broadcast.269.clone, s32[64]{0:T(128)S(1)} %get-tuple-element.48, bf16[64,128,128]{2,1,0:T(8,128)(2,1)} %all-gather.3.cloned.1.call-done), kind=kCustom, calls=%fused_computation.14 | custom fusion | bytes 6291712 | tf_op jit(solution)/shard_map/scatter | solution.py:31
  109.2 3.5 all-to-all-start.3
  112.7 6.5 %fusion.63 = bf16[64,128,128]{2,1,0:T(8,128)(2,1)} fusion(bf16[64,256,128]{2,1,0:T(8,128)(2,1)} %param.23, bf16[64,256,128]{2,1,0:T(8,128)(2,1)} %gather_fusion.4, pred[64]{0:T(512)(128)(4,1)S(1)} %copy-done.19), kind=kOutput, calls=%fused_computation.66 | convolution fusion | flops 540016640 | bytes 10485824 | tf_op jit(solution)/shard_map/pvn,pvm->pnm/dot_general | solution.py:119
  119.2 0.9 broadcast.269.clone.1
  120.1 9.5 %scatter_fusion.1 = bf16[16,128,128]{2,1,0:T(8,128)(2,1)} fusion(bf16[16,128,128]{2,1,0:T(8,128)(2,1)} %broadcast.269.clone.1, s32[64]{0:T(128)S(1)} %get-tuple-element.47, bf16[64,128,128]{2,1,0:T(8,128)(2,1)S(1)} %copy-done.1), kind=kCustom, calls=%fused_computation.12 | custom fusion | bytes 6291712 | tf_op jit(solution)/shard_map/scatter | solution.py:31
  129.7 3.7 all-to-all-start.1
  133.4 6.4 %fusion.60 = bf16[64,128,128]{2,1,0:T(8,128)(2,1)} fusion(bf16[64,256,128]{2,1,0:T(8,128)(2,1)} %param.23, bf16[64,256,128]{2,1,0:T(8,128)(2,1)} %gather_fusion.2, pred[64]{0:T(512)(128)(4,1)S(1)} %copy-done.21), kind=kOutput, calls=%fused_computation.65 | convolution fusion | flops 540016640 | bytes 10485824 | tf_op jit(solution)/shard_map/pvn,pvm->pnm/dot_general | solution.py:119
  139.8 0.9 broadcast.269.clone.2
  140.7 10.5 %scatter_fusion.5 = bf16[16,128,128]{2,1,0:T(8,128)(2,1)} fusion(bf16[16,128,128]{2,1,0:T(8,128)(2,1)} %broadcast.269.clone.2, s32[64]{0:T(128)S(1)} %get-tuple-element.31, bf16[64,128,128]{2,1,0:T(8,128)(2,1)S(1)} %copy-done.1), kind=kCustom, calls=%fused_computation.16 | custom fusion | bytes 6291712 | tf_op jit(solution)/shard_map/scatter | solution.py:31
  151.2 4.1 all-to-all-start.5
  155.4 6.4 %fusion.66 = bf16[64,128,128]{2,1,0:T(8,128)(2,1)} fusion(bf16[64,256,128]{2,1,0:T(8,128)(2,1)} %param.23, bf16[64,256,128]{2,1,0:T(8,128)(2,1)} %gather_fusion.6, pred[64]{0:T(512)(128)(4,1)S(1)} %get-tuple-element.16), kind=kOutput, calls=%fused_computation.67 | convolution fusion | flops 540016640 | bytes 10485824 | tf_op jit(solution)/shard_map/pvn,pvm->pnm/dot_general | solution.py:119
  161.8 2.2 gather_fusion.5
  164.0 2.2 gather_fusion.3
  166.1 3.2 gather_fusion.7
  169.3 6.3 %fusion.38 = f32[64,128,128]{2,1,0:T(8,128)} fusion(bf16[64,128,128]{2,1,0:T(8,128)(2,1)} %fusion.63, bf16[64,128,128]{2,1,0:T(8,128)(2,1)} %gather_fusion.5, pred[64]{0:T(512)(128)(4,1)S(1)} %copy-done.19), kind=kOutput, calls=%fused_computation.52 | convolution fusion | flops 538968064 | bytes 8388672 | tf_op jit(solution)/shard_map/pac,pdc->pad/dot_general | solution.py:44
  175.6 6.3 %fusion.44 = f32[64,128,128]{2,1,0:T(8,128)} fusion(bf16[64,128,128]{2,1,0:T(8,128)(2,1)} %fusion.60, bf16[64,128,128]{2,1,0:T(8,128)(2,1)} %gather_fusion.3, pred[64]{0:T(512)(128)(4,1)S(1)} %copy-done.21), kind=kOutput, calls=%fused_computation.54 | convolution fusion | flops 538968064 | bytes 8388672 | tf_op jit(solution)/shard_map/pac,pdc->pad/dot_general | solution.py:44
  182.0 9.0 %multiply_add_fusion.1 = f32[64,128,128]{2,1,0:T(8,128)} fusion(f32[64,128,128]{2,1,0:T(8,128)} %fusion.38, f32[64,128,128]{2,1,0:T(8,128)} %fusion.44, bf16[64,128,128]{2,1,0:T(8,128)(2,1)} %fusion.66, f32[64]{0:T(128)S(1)} %get-tuple-element.25, f32[64]{0:T(128)S(1)} %get-tuple-element.26, f32[64]{0:T(128)S(1)} %get-tuple-element.24, ...), kind=kOutput, calls=%fused_computation.27 | convolution fusion | flops 544210944 | bytes 16778048 | tf_op jit(solution)/shard_map/pac,pdc->pad/dot_general | solution.py:44
  191.3 5.4 %copy.48 = bf16[64,128,128]{0,2,1:T(8,128)(2,1)} copy(bf16[64,128,128]{2,1,0:T(8,128)(2,1)} %param.24) | data formatting | bytes 4194304 | tf_op args[9]
  196.6 2.0 gather_fusion.1
  198.8 2.3 gather_fusion
  201.9 2.0 convolution_add_fusion.3
  204.0 65.8 %reduce-scatter.6.cloned.1.call-done = f32[64,32,128]{2,1,0:T(8,128)} async-done(((f32[64,128,128]{2,1,0:T(8,128)}), f32[64,32,128]{2,1,0:T(8,128)}) %reduce-scatter.6.cloned.1.call-update) | async-done | bytes 1048592 | tf_op jit(solution)/shard_map/reduce_scatter | solution.py:137
  269.8 4.2 fusion.143
  274.1 46.6 %all-gather.5.cloned.1.call-done = bf16[64,128,128]{2,1,0:T(8,128)(2,1)} async-done(((bf16[64,32,128]{2,1,0:T(8,128)(2,1)}), bf16[64,128,128]{2,1,0:T(8,128)(2,1)}) %all-gather.5.cloned.1.call-update) | async-done | bytes 2097168 | tf_op jit(solution)/shard_map/all_gather | solution.py:154
  320.7 0.9 broadcast.269.clone.4
  321.6 10.0 %scatter_fusion.6 = bf16[16,128,128]{2,1,0:T(8,128)(2,1)} fusion(bf16[16,128,128]{2,1,0:T(8,128)(2,1)} %broadcast.269.clone.4, s32[64]{0:T(128)S(1)} %get-tuple-element.47, bf16[64,128,128]{2,1,0:T(8,128)(2,1)} %all-gather.5.cloned.1.call-done), kind=kCustom, calls=%fused_computation.17 | custom fusion | bytes 6291712 | tf_op jit(solution)/shard_map/scatter | solution.py:31
  331.6 3.5 all-to-all-start.6
  335.1 0.9 broadcast.269.clone.3
  336.0 9.4 %scatter_fusion.7 = bf16[16,128,128]{2,1,0:T(8,128)(2,1)} fusion(bf16[16,128,128]{2,1,0:T(8,128)(2,1)} %broadcast.269.clone.3, s32[64]{0:T(128)S(1)} %get-tuple-element.48, bf16[64,128,128]{2,1,0:T(8,128)(2,1)S(1)} %copy-done.3), kind=kCustom, calls=%fused_computation.18 | custom fusion | bytes 6291712 | tf_op jit(solution)/shard_map/scatter | solution.py:31
  345.4 0.9 broadcast.269.clone.5
  346.3 9.2 %scatter_fusion.8 = bf16[16,128,128]{2,1,0:T(8,128)(2,1)} fusion(bf16[16,128,128]{2,1,0:T(8,128)(2,1)} %broadcast.269.clone.5, s32[64]{0:T(128)S(1)} %get-tuple-element.31, bf16[64,128,128]{2,1,0:T(8,128)(2,1)S(1)} %copy-done.3), kind=kCustom, calls=%fused_computation.19 | custom fusion | bytes 6291712 | tf_op jit(solution)/shard_map/scatter | solution.py:31
  355.5 4.0 all-to-all-start.7
  359.5 2.4 gather_fusion.8
  361.9 5.0 %fusion.31 = f32[64,128,128]{2,1,0:T(8,128)} fusion(bf16[64,128,128]{2,1,0:T(8,128)(2,1)S(1)} %copy-done.6, bf16[64,128,128]{2,1,0:T(8,128)(2,1)} %gather_fusion.8, pred[64]{0:T(512)(128)(4,1)S(1)} %copy-done.22), kind=kOutput, calls=%fused_computation.49 | convolution fusion | flops 538968064 | bytes 8388672 | tf_op jit(solution)/shard_map/pac,pdc->pad/dot_general | solution.py:44
  367.0 2.3 all-to-all-done.7
  369.2 3.5 all-to-all-start.8
  373.1 2.4 gather_fusion.9
  375.5 5.0 %fusion.25 = f32[64,128,128]{2,1,0:T(8,128)} fusion(bf16[64,128,128]{2,1,0:T(8,128)(2,1)S(1)} %copy-done.5, bf16[64,128,128]{2,1,0:T(8,128)(2,1)} %gather_fusion.9, pred[64]{0:T(512)(128)(4,1)S(1)} %copy-done.20), kind=kOutput, calls=%fused_computation.47 | convolution fusion | flops 538968064 | bytes 8388672 | tf_op jit(solution)/shard_map/pac,pdc->pad/dot_general | solution.py:44
  380.5 1.9 all-to-all-done.8
  382.4 2.1 gather_fusion.10
  384.6 7.8 %multiply_add_fusion = f32[64,128,128]{2,1,0:T(8,128)} fusion(f32[64,128,128]{2,1,0:T(8,128)} %fusion.25, f32[64,128,128]{2,1,0:T(8,128)} %fusion.31, bf16[64,128,128]{2,1,0:T(8,128)(2,1)S(1)} %copy-done.2, f32[64]{0:T(128)S(1)} %copy-done.14, f32[64]{0:T(128)S(1)} %copy-done.16, f32[64]{0:T(128)S(1)} %copy-done.12, ...), kind=kOutput, calls=%fused_computation.26 | convolution fusion | flops 544210944 | bytes 16778048 | tf_op jit(solution)/shard_map/pac,pdc->pad/dot_general | solution.py:44
  392.5 1.6 copy-done.4
  394.3 2.9 convolution_add_fusion.1
  397.2 68.6 %reduce-scatter.8.cloned.1.call-done = f32[64,32,128]{2,1,0:T(8,128)} async-done(((f32[64,128,128]{2,1,0:T(8,128)}), f32[64,32,128]{2,1,0:T(8,128)}) %reduce-scatter.8.cloned.1.call-update) | async-done | bytes 1048592 | tf_op jit(solution)/shard_map/reduce_scatter | solution.py:137
  465.8 4.3 multiply_multiply_fusion
  (106 shorter events, 6.4 us)
Async XLA Ops:
  6.5 72.1 %copy-start = (f32[256,256]{1,0:T(8,128)S(1)}, f32[256,256]{1,0:T(8,128)}, u32[]{:S(2)}) copy-start(f32[256,256]{1,0:T(8,128)} %param.20) | copy-start | bytes 786436
  6.5 90.5 %all-gather.3.cloned.1.call-start = ((), (), s32[]{:S(2)}) async-start(), calls=%async_computation.13 | async-start | bytes 2621440 | tf_op jit(solution)/shard_map/all_gather | solution.py:96
  9.8 192.1 %reduce-scatter.4.cloned.1.call-start = ((), (), s32[]{:S(2)}) async-start(), calls=%async_computation.12 | async-start | bytes 5242880 | tf_op jit(solution)/shard_map/reduce_scatter | solution.py:94
  19.9 0.7 copy-start.8
  36.1 20.1 %all-to-all-start.2 = ((bf16[8,2,256,128]{3,2,1,0:T(8,128)(2,1)}), bf16[8,2,256,128]{3,2,1,0:T(8,128)(2,1)S(1)}, u32[]{:S(2)}, u32[]{:S(2)}) async-start(bf16[8,2,256,128]{3,2,1,0:T(8,128)(2,1)} %bitcast.17), calls=%async_computation.3 | async-start | bytes 2097152 | tf_op jit(solution)/shard_map/all_to_all | solution.py:107
  54.4 5.3 %copy-start.23 = (s32[64,2]{0,1:T(2,128)S(1)}, s32[64,2]{0,1:T(2,128)}, u32[]{:S(2)}) copy-start(s32[64,2]{0,1:T(2,128)} %param.15) | copy-start | bytes 1540
  54.4 5.3 %copy-start.26 = (s32[64,3]{0,1:T(4,128)S(1)}, s32[64,3]{0,1:T(4,128)}, u32[]{:S(2)}) copy-start(s32[64,3]{0,1:T(4,128)} %param.19) | copy-start | bytes 2308
  54.4 5.6 %copy-start.25 = (s32[64,3]{0,1:T(4,128)S(1)}, s32[64,3]{0,1:T(4,128)}, u32[]{:S(2)}) copy-start(s32[64,3]{0,1:T(4,128)} %param.18) | copy-start | bytes 2308
  56.2 18.9 %all-to-all-start = ((bf16[8,2,256,128]{3,2,1,0:T(8,128)(2,1)}), bf16[8,2,256,128]{3,2,1,0:T(8,128)(2,1)S(1)}, u32[]{:S(2)}, u32[]{:S(2)}) async-start(bf16[8,2,256,128]{3,2,1,0:T(8,128)(2,1)} %bitcast.8), calls=%async_computation.1 | async-start | bytes 2097152 | tf_op jit(solution)/shard_map/all_to_all | solution.py:107
  74.1 5.1 %copy-start.27 = (s32[64]{0:T(128)S(1)}, s32[64]{0:T(128)}, u32[]{:S(2)}) copy-start(s32[64]{0:T(128)} %get-tuple-element.14) | copy-start | bytes 772
  74.1 5.1 %copy-start.28 = (s32[64]{0:T(128)S(1)}, s32[64]{0:T(128)}, u32[]{:S(2)}) copy-start(s32[64]{0:T(128)} %get-tuple-element.54) | copy-start | bytes 772
  75.1 18.9 %all-to-all-start.4 = ((bf16[8,2,256,128]{3,2,1,0:T(8,128)(2,1)}), bf16[8,2,256,128]{3,2,1,0:T(8,128)(2,1)S(1)}, u32[]{:S(2)}, u32[]{:S(2)}) async-start(bf16[8,2,256,128]{3,2,1,0:T(8,128)(2,1)} %bitcast.26), calls=%async_computation.5 | async-start | bytes 2097152 | tf_op jit(solution)/shard_map/all_to_all | solution.py:107
  80.4 101.5 %copy-start.17 = (pred[64]{0:T(512)(128)(4,1)}, pred[64]{0:T(512)(128)(4,1)S(1)}, u32[]{:S(2)}) copy-start(pred[64]{0:T(512)(128)(4,1)S(1)} %get-tuple-element.16) | copy-start | bytes 196
  80.4 81.4 %copy-start.9 = (s32[1024]{0:T(1024)}, s32[1024]{0:T(1024)S(1)}, u32[]{:S(2)}) copy-start(s32[1024]{0:T(1024)S(1)} %pad_clamp_fusion.1) | copy-start | bytes 12292
  80.5 83.5 %copy-start.10 = (s32[1024]{0:T(1024)}, s32[1024]{0:T(1024)S(1)}, u32[]{:S(2)}) copy-start(s32[1024]{0:T(1024)S(1)} %pad_clamp_fusion.2) | copy-start | bytes 12292
  80.7 101.3 %copy-start.11 = (f32[64]{0:T(128)}, f32[64]{0:T(128)S(1)}, u32[]{:S(2)}) copy-start(f32[64]{0:T(128)S(1)} %get-tuple-element.24) | copy-start | bytes 772
  80.7 101.3 %copy-start.13 = (f32[64]{0:T(128)}, f32[64]{0:T(128)S(1)}, u32[]{:S(2)}) copy-start(f32[64]{0:T(128)S(1)} %get-tuple-element.25) | copy-start | bytes 772
  80.7 101.3 %copy-start.15 = (f32[64]{0:T(128)}, f32[64]{0:T(128)S(1)}, u32[]{:S(2)}) copy-start(f32[64]{0:T(128)S(1)} %get-tuple-element.26) | copy-start | bytes 772
  98.0 14.7 %copy-start.19 = (pred[64]{0:T(512)(128)(4,1)S(1)}, pred[64]{0:T(512)(128)(4,1)}, u32[]{:S(2)}) copy-start(pred[64]{0:T(512)(128)(4,1)} %get-tuple-element.27) | copy-start | bytes 196
  109.2 20.5 %all-to-all-start.3 = ((bf16[8,2,128,128]{3,2,1,0:T(8,128)(2,1)}), bf16[8,2,128,128]{3,2,1,0:T(8,128)(2,1)S(1)}, u32[]{:S(2)}, u32[]{:S(2)}) async-start(bf16[8,2,128,128]{3,2,1,0:T(8,128)(2,1)} %bitcast.19), calls=%async_computation.4 | async-start | bytes 1048576 | tf_op jit(solution)/shard_map/all_to_all | solution.py:110
  112.7 7.5 %copy-start.1 = (bf16[64,128,128]{2,1,0:T(8,128)(2,1)S(1)}, bf16[64,128,128]{2,1,0:T(8,128)(2,1)}, u32[]{:S(2)}) copy-start(bf16[64,128,128]{2,1,0:T(8,128)(2,1)} %all-gather.3.cloned.1.call-done) | copy-start | bytes 6291460
  120.1 13.2 %copy-start.21 = (pred[64]{0:T(512)(128)(4,1)S(1)}, pred[64]{0:T(512)(128)(4,1)}, u32[]{:S(2)}) copy-start(pred[64]{0:T(512)(128)(4,1)} %get-tuple-element.29) | copy-start | bytes 196
  129.7 21.5 %all-to-all-start.1 = ((bf16[8,2,128,128]{3,2,1,0:T(8,128)(2,1)}), bf16[8,2,128,128]{3,2,1,0:T(8,128)(2,1)S(1)}, u32[]{:S(2)}, u32[]{:S(2)}) async-start(bf16[8,2,128,128]{3,2,1,0:T(8,128)(2,1)} %bitcast.10), calls=%async_computation.2 | async-start | bytes 1048576 | tf_op jit(solution)/shard_map/all_to_all | solution.py:110
  151.2 14.9 %all-to-all-start.5 = ((bf16[8,2,128,128]{3,2,1,0:T(8,128)(2,1)}), bf16[8,2,128,128]{3,2,1,0:T(8,128)(2,1)}, u32[]{:S(2)}, u32[]{:S(2)}) async-start(bf16[8,2,128,128]{3,2,1,0:T(8,128)(2,1)} %bitcast.28), calls=%async_computation.6 | async-start | bytes 1048576 | tf_op jit(solution)/shard_map/all_to_all | solution.py:110
  155.4 114.4 %reduce-scatter.6.cloned.1.call-start = ((), (), s32[]{:S(2)}) async-start(), calls=%async_computation.14 | async-start | bytes 5242880 | tf_op jit(solution)/shard_map/reduce_scatter | solution.py:137
  191.0 10.2 %copy-start.24 = (s32[64,2]{0,1:T(2,128)S(1)}, s32[64,2]{0,1:T(2,128)}, u32[]{:S(2)}) copy-start(s32[64,2]{0,1:T(2,128)} %param.15) | copy-start | bytes 1540
  191.0 129.7 %all-gather.5.cloned.1.call-start = ((), (), s32[]{:S(2)}) async-start(), calls=%async_computation.15 | async-start | bytes 2621440 | tf_op jit(solution)/shard_map/all_gather | solution.py:154
  321.6 14.4 %copy-start.3 = (bf16[64,128,128]{2,1,0:T(8,128)(2,1)S(1)}, bf16[64,128,128]{2,1,0:T(8,128)(2,1)}, u32[]{:S(2)}) copy-start(bf16[64,128,128]{2,1,0:T(8,128)(2,1)} %all-gather.5.cloned.1.call-done) | copy-start | bytes 6291460
  331.6 23.9 %all-to-all-start.6 = ((bf16[8,2,128,128]{3,2,1,0:T(8,128)(2,1)}), bf16[8,2,128,128]{3,2,1,0:T(8,128)(2,1)S(1)}, u32[]{:S(2)}, u32[]{:S(2)}) async-start(bf16[8,2,128,128]{3,2,1,0:T(8,128)(2,1)} %bitcast.33), calls=%async_computation.8 | async-start | bytes 1048576 | tf_op jit(solution)/shard_map/all_to_all | solution.py:129
  355.5 13.8 %all-to-all-start.7 = ((bf16[8,2,128,128]{3,2,1,0:T(8,128)(2,1)}), bf16[8,2,128,128]{3,2,1,0:T(8,128)(2,1)S(1)}, u32[]{:S(2)}, u32[]{:S(2)}) async-start(bf16[8,2,128,128]{3,2,1,0:T(8,128)(2,1)} %bitcast.35), calls=%async_computation.9 | async-start | bytes 1048576 | tf_op jit(solution)/shard_map/all_to_all | solution.py:129
  359.5 2.4 copy-start.6
  359.5 2.4 copy-start.22
  369.2 13.2 %all-to-all-start.8 = ((bf16[8,2,128,128]{3,2,1,0:T(8,128)(2,1)}), bf16[8,2,128,128]{3,2,1,0:T(8,128)(2,1)S(1)}, u32[]{:S(2)}, u32[]{:S(2)}) async-start(bf16[8,2,128,128]{3,2,1,0:T(8,128)(2,1)} %bitcast.37), calls=%async_computation.10 | async-start | bytes 1048576 | tf_op jit(solution)/shard_map/all_to_all | solution.py:129
  372.7 93.1 %reduce-scatter.8.cloned.1.call-start = ((), (), s32[]{:S(2)}) async-start(), calls=%async_computation.16 | async-start | bytes 5242880 | tf_op jit(solution)/shard_map/reduce_scatter | solution.py:137
  373.1 2.4 copy-start.5
  373.1 2.4 copy-start.20
  382.4 2.2 copy-start.2
  382.4 2.2 copy-start.12
  382.4 2.2 copy-start.14
  382.4 2.2 copy-start.16
  382.4 2.2 copy-start.18
  392.5 1.6 copy-start.4
  392.5 1.9 copy-start.7
  394.3 71.5 %copy-start.29 = (f32[64]{0:T(128)S(1)}, f32[64]{0:T(128)}, u32[]{:S(2)}) copy-start(f32[64]{0:T(128)} %select_reduce_fusion) | copy-start | bytes 772
Sparse Core Ops, SparseCore 0:
  9.9 48.6 all-gather.2
  60.9 75.4 reduce-scatter.3
  191.1 78.6 reduce-scatter.5
  274.2 46.4 all-gather.4
  392.6 73.1 reduce-scatter.7
where the time goes:
time: 479 us; the launch traced here: 477 us
  waiting for transfers between devices  195 us (41%)
  local copies, waits for them, and re-layouts  143 us (30%)
  matrix products  82.7 us (17%)
  starting transfers between devices  34.8 us (7%)
  between operations  13.6 us (3%)
  other arithmetic  6.82 us (1%)
    reduce_scatter x2, waiting for transfers between devices, per_device(): lax.psum_scatter(coupling, 'aux', scatter_dimension=1, tiled=True)  134 us
    scatter x9, local copies, waits for them, and re-layouts, pack_slots(): filled = blank_buffer.at[send_place].set(values, mode='drop')  97.6 us
    all_gather x2, waiting for transfers between devices, per_device(): lax.all_gather(amps_rows.astype(jnp.bfloat16), 'aux', axis=1, tiled=True)  46.6 us
    dot_general x6, matrix products, coupled_term(): jnp.einsum('pac,pdc->pad', mixed_amp, projector, preferred_element_type=j...  39.5 us
    gather x9, local copies, waits for them, and re-layouts, read_slots(): return jnp.take(flattened, read_place, axis=0)  23.6 us
    all_to_all x6, starting transfers between devices, per_device(): lax.all_to_all(amps_buffer, 'pairs', split_axis=0, concat_axis=0, tiled=T...  22.3 us
    dot_general x3, matrix products, per_device(): jnp.einsum('pvn,pvm->pnm', pno_coef, far_coef, preferred_element_type=jnp...  19.3 us
    all_to_all x3, starting transfers between devices, per_device(): lax.all_to_all(coef_buffer, 'pairs', split_axis=0, concat_axis=0, tiled=T...  11.8 us
  transfers between devices with their start and end apart: 14, of which 8 were waited for; matrix products, arithmetic and copies ran while one was open for 41% of the time, Pallas kernels for 0%

commit v1 on v0

v1 whole, which is shorter than its diff:
```python
import functools

import jax
import jax.numpy as jnp
from jax import lax
from jax.experimental import pallas as pl
from jax.experimental.pallas import tpu as pltpu
from jax.sharding import PartitionSpec as P

MOST = 2
VMEM_BYTES = 48 * 1024 * 1024

SMEM = pl.BlockSpec(memory_space=pltpu.SMEM)
VMEM = pl.BlockSpec(memory_space=pltpu.VMEM)
ANY = pl.BlockSpec(memory_space=pl.ANY)
HBM = pl.BlockSpec(memory_space=pltpu.HBM)
precise = lax.Precision.HIGHEST


def dot(left, right, over_left, over_right):
    return lax.dot_general(
        left, right, (((over_left,), (over_right,)), ((), ())), preferred_element_type=jnp.float32
    )


def params():
    return pltpu.CompilerParams(vmem_limit_bytes=VMEM_BYTES)


def pair_places(partner, pair_dev, dev_count):
    slots = partner.shape[1]
    owner = jnp.where(partner >= 0, partner // pair_dev, -1)
    own_id = jnp.broadcast_to(jnp.arange(pair_dev, dtype=jnp.int32)[:, None], partner.shape)
    far_key = (partner - owner * pair_dev) * pair_dev + own_id
    none = pair_dev * pair_dev
    devs = jnp.arange(dev_count, dtype=jnp.int32)[None, :, None]
    hit = owner[:, None, :] == devs

    def ranked(key):
        left = jnp.where(hit, key[:, None, :], none)
        found = []
        for _ in range(MOST):
            least = jnp.min(left, axis=0)
            found.append(least)
            left = jnp.where(left == least[None], none, left)
        return jnp.stack(found, axis=-1).reshape(-1)

    send = ranked(own_id)
    read = ranked(far_key)
    send = jnp.where(send < none, send, 0)
    read = jnp.where(read < none, lax.rem(read, pair_dev), -1)
    return send, read


def pack_rows(send_ref, half_ref, out_ref):
    def body(item, carry):
        out_ref[item] = half_ref[send_ref[item]]
        return carry

    lax.fori_loop(0, out_ref.shape[0], body, 0, unroll=4)


def start_kernel(place_ref, send_ref, count_ref, amps_ref, kept_ref, half_ref, out_ref):
    pairs, rows, width = amps_ref.shape
    row_id = lax.broadcasted_iota(jnp.int32, (rows, width), 0) + place_ref[1] * rows
    col_id = lax.broadcasted_iota(jnp.int32, (rows, width), 1)
    last = jnp.maximum(row_id, col_id)

    def body(pair, carry):
        kept = jnp.where(last < count_ref[pair], amps_ref[pair], 0.0)
        kept_ref[pair] = kept
        half_ref[pair] = kept.astype(jnp.bfloat16)
        return carry

    lax.fori_loop(0, pairs, body, 0, unroll=4)
    pack_rows(send_ref, half_ref, out_ref)


def coef_kernel(slots, place_ref, send_ref, coef_ref, *rest):
    outs, (held, in_sems, out_sems) = rest[:-3], rest[-3:]
    per_dev = slots * MOST

    def fetch(turn, item):
        far = place_ref[0] ^ (turn + 1)
        pair = send_ref[far * per_dev + item]
        place = turn * per_dev + item
        return pltpu.make_async_copy(coef_ref.at[pair], held.at[place], in_sems.at[place])

    def store(turn):
        return pltpu.make_async_copy(
            held.at[pl.ds(turn * per_dev, per_dev)], outs[turn], out_sems.at[turn]
        )

    for turn in range(len(outs)):
        for item in range(per_dev):
            fetch(turn, item).start()
    for turn in range(len(outs)):
        for item in range(per_dev):
            fetch(turn, item).wait()
        store(turn).start()
    for turn in range(len(outs)):
        store(turn).wait()


def left_part(fock_rows, half_rows):
    return dot(fock_rows, half_rows, 0, 0)


def prepare_kernel(
    place_ref, count_ref, energy_ref, left_ref, right_ref, fock_ref, kept_ref, half_ref,
    part_ref, scale_ref, own_ref,
):
    block, rows, width = kept_ref.shape
    first = pl.program_id(0) * block
    row_start = pl.multiple_of(place_ref[1] * rows, rows)
    row_id = lax.broadcasted_iota(jnp.int32, (rows, width), 0) + row_start
    col_id = lax.broadcasted_iota(jnp.int32, (rows, width), 1)
    last = jnp.maximum(row_id, col_id)
    eye_rows = row_id == col_id
    eye = lax.broadcasted_iota(jnp.int32, (width, width), 0) == lax.broadcasted_iota(
        jnp.int32, (width, width), 1
    )
    for pair in range(block):
        energy = energy_ref[first + pair]
        fock = fock_ref[pair]
        fock_rows = fock_ref[pair, pl.ds(row_start, rows), :]
        half = half_ref[pair]
        part_ref[pair] = dot(left_ref[pair], right_ref[pair], 1, 1) + left_part(fock_rows, half)
        own_ref[pair] = dot(half, fock, 1, 0) - energy * kept_ref[pair]
        diag_cols = jnp.sum(jnp.where(eye, fock.astype(jnp.float32), 0.0), axis=0, keepdims=True)
        diag_rows = jnp.sum(
            jnp.where(eye_rows, fock_rows.astype(jnp.float32), 0.0), axis=1, keepdims=True
        )
        denominator = diag_rows + diag_cols - energy
        scale_ref[pair] = jnp.where(last < count_ref[first + pair], 1.0 / denominator, 0.0)


def projector_kernel(slots, place_ref, read_ref, coef_ref, *rest):
    arrived, out_ref = rest[:-1], rest[-1]
    per_dev = slots * MOST
    for turn in range(len(arrived)):
        far = place_ref[0] ^ (turn + 1)
        for item in range(per_dev):
            pair = read_ref[far * per_dev + item]
            own = coef_ref[jnp.maximum(pair, 0)]
            out_ref[turn * per_dev + item] = dot(own, arrived[turn][item], 0, 0).astype(
                jnp.bfloat16
            )


def add_coupling(slots, all_slots, place_ref, read_ref, weight_ref, proj_ref, amps_ref, part_ref):
    per_dev = slots * MOST
    width = proj_ref.shape[-1]

    def body(turn, carry):
        far = place_ref[0] ^ (turn + 1)
        terms = []
        for item in range(per_dev):
            slot = place_ref[1] * slots + item // MOST
            pair = read_ref[(far * all_slots + slot) * MOST + item % MOST]
            safe = jnp.maximum(pair, 0)
            weight = jnp.where(pair >= 0, weight_ref[safe * all_slots + slot], 0.0)
            proj = proj_ref[turn * per_dev + item]
            amps = amps_ref[far, :, item].reshape(width, width)
            mixed = dot(proj, amps, 1, 0).astype(jnp.bfloat16)
            terms.append((safe, weight * dot(mixed, proj, 1, 1)))
        for safe, term in terms:
            part_ref[safe] += term
        return carry

    lax.fori_loop(0, proj_ref.shape[0] // per_dev, body, 0)


def coupling_kernel(
    slots, all_slots, scaled, place_ref, read_ref, weight_ref, proj_ref, amps_ref, start_ref,
    out_ref, own_ref, part_ref,
):
    part_ref[...] = jnp.zeros_like(part_ref)
    add_coupling(slots, all_slots, place_ref, read_ref, weight_ref, proj_ref, amps_ref, part_ref)
    pairs, rows, width = own_ref.shape
    parts = width // rows
    row_start = pl.multiple_of(place_ref[1] * rows, rows)

    if not scaled:

        def body(pair, carry):
            total = (part_ref[pair] + start_ref[pair]).astype(out_ref.dtype)
            for part in range(parts):
                out_ref[part, pair] = total[part * rows : (part + 1) * rows]
            at = pl.ds(row_start, rows)
            own_ref[pair] = part_ref[pair, at] + start_ref[pair, at]
            return carry

        lax.fori_loop(0, pairs, body, 0, unroll=2)
        return

    def body(pair, most):
        total = part_ref[pair] + start_ref[pair]
        for part in range(parts):
            piece = total[part * rows : (part + 1) * rows]
            out_ref[part, pair] = piece
            most = jnp.maximum(most, jnp.abs(piece))
        at = pl.ds(row_start, rows)
        own_ref[pair] = part_ref[pair, at] + start_ref[pair, at]
        return most

    most = lax.fori_loop(0, pairs, body, jnp.zeros((rows, width), jnp.float32), unroll=2)
    most = jnp.max(jnp.max(most, axis=0, keepdims=True), axis=1, keepdims=True)
    power = jnp.maximum(jnp.ceil(jnp.log2(jnp.maximum(most, 1.0)) - 15.0), 0.0)
    for part in range(parts):
        out_ref[part, pairs] = jnp.broadcast_to(power, (rows, width))


def first_update_kernel(
    send_ref, sum_ref, own_ref, scale_ref, kept_ref, new_ref, half_ref, out_ref
):
    def body(pair, carry):
        new = kept_ref[pair] - (sum_ref[pair] + own_ref[pair]) * scale_ref[pair]
        new_ref[pair] = new
        half_ref[pair] = new.astype(jnp.bfloat16)
        return carry

    lax.fori_loop(0, new_ref.shape[0], body, 0, unroll=4)
    pack_rows(send_ref, half_ref, out_ref)


def between_kernel(
    place_ref, energy_ref, fock_ref, kept_ref, half_ref, before_ref, sum_ref, old_ref,
    part_ref, own_ref,
):
    block, rows, width = kept_ref.shape
    first = pl.program_id(0) * block
    row_start = pl.multiple_of(place_ref[1] * rows, rows)
    for pair in range(block):
        half = half_ref[pair]
        fock_rows = fock_ref[pair, pl.ds(row_start, rows), :]
        part_ref[pair] = (
            left_part(fock_rows, half) - left_part(fock_rows, before_ref[pair]) - old_ref[pair]
        )
        own_ref[pair] = (
            dot(half, fock_ref[pair], 1, 0)
            - energy_ref[first + pair] * kept_ref[pair]
            + sum_ref[pair]
        )


def last_update_kernel(place_ref, got_ref, mine_ref, own_ref, scale_ref, kept_ref, new_ref):
    def body(pair, carry):
        total = mine_ref[pair]
        for turn in range(1, got_ref.shape[0]):
            part = lax.rem(place_ref[1] + turn, got_ref.shape[0])
            total = total + got_ref[part, pair].astype(jnp.float32)
        new_ref[pair] = kept_ref[pair] - (total + own_ref[pair]) * scale_ref[pair]
        return carry

    lax.fori_loop(0, new_ref.shape[0], body, 0, unroll=4)


def shape(dims, dtype):
    return jax.ShapeDtypeStruct(tuple(dims), dtype)


def per_device(
    pair_orbits,
    pno_count,
    partner,
    couple_orbit,
    couple_side,
    occ_fock,
    fit_left,
    fit_right,
    pno_coef,
    virt_fock,
    amps_in,
):
    pair_dev = pno_count.shape[0]
    width = virt_fock.shape[1]
    rows = amps_in.shape[1]
    slots = partner.shape[1]
    dev_count = lax.axis_size("pairs")
    aux_count = lax.axis_size("aux")
    all_slots = slots * aux_count
    per_dev = slots * MOST
    bf16, f32 = jnp.bfloat16, jnp.float32
    place = jnp.stack([lax.axis_index("pairs"), lax.axis_index("aux")]).astype(jnp.int32)

    coef_send, coef_read = pair_places(partner, pair_dev, dev_count)

    coef_out = pl.pallas_call(
        functools.partial(coef_kernel, slots),
        out_shape=tuple(
            shape((per_dev,) + pno_coef.shape[1:], bf16) for _ in range(dev_count - 1)
        ),
        in_specs=[SMEM, SMEM, ANY],
        out_specs=tuple(HBM for _ in range(dev_count - 1)),
        scratch_shapes=[
            pltpu.VMEM(((dev_count - 1) * per_dev,) + pno_coef.shape[1:], bf16),
            pltpu.SemaphoreType.DMA(((dev_count - 1) * per_dev,)),
            pltpu.SemaphoreType.DMA((dev_count - 1,)),
        ],
        compiler_params=params(),
        name="pack_coef",
    )(place, coef_send, pno_coef)

    tables = jnp.concatenate([partner, couple_orbit, couple_side], axis=1)
    tables, coef_out = lax.optimization_barrier((tables, coef_out))
    coef_far = [
        lax.ppermute(coef_out[turn], "pairs", [(dev, dev ^ (turn + 1)) for dev in range(dev_count)])
        for turn in range(dev_count - 1)
    ]

    shares = [tables] + [
        lax.ppermute(tables, "aux", [(dev, (dev + turn) % aux_count) for dev in range(aux_count)])
        for turn in range(1, aux_count)
    ]
    tables = jnp.zeros((aux_count,) + tables.shape, jnp.int32)
    owners = jnp.arange(aux_count)[:, None, None]
    for turn, share in enumerate(shares):
        owner = lax.rem(place[1] + aux_count - turn, aux_count)
        tables = jnp.where(owners == owner, share[None], tables)
    tables = tables.reshape(aux_count, pair_dev, 3, slots).transpose(2, 1, 0, 3)
    tables = tables.reshape(3, pair_dev, all_slots)
    partner, couple_orbit, couple_side = tables[0], tables[1], tables[2]
    send, read = pair_places(partner, pair_dev, dev_count)

    occ_ids = jnp.arange(occ_fock.shape[0], dtype=jnp.int32)
    occ_diag = jnp.diagonal(occ_fock)
    energy = jnp.sum(
        jnp.where(pair_orbits[:, :, None] == occ_ids[None, None, :], occ_diag[None, None, :], 0.0),
        axis=(1, 2),
    )
    free_orbit = jnp.where(couple_side == 0, pair_orbits[:, 0:1], pair_orbits[:, 1:2])
    onehot = (couple_orbit.reshape(-1)[:, None] == occ_ids[None, :]).astype(f32)
    fock_rows = jnp.dot(onehot, occ_fock, precision=precise)
    weight = -jnp.sum(
        jnp.where(free_orbit.reshape(-1)[:, None] == occ_ids[None, :], fock_rows, 0.0), axis=1
    )

    places = dev_count * all_slots * MOST
    kept, half, amps_out = pl.pallas_call(
        start_kernel,
        out_shape=(
            shape(amps_in.shape, f32),
            shape(amps_in.shape, bf16),
            shape((places, rows, width), bf16),
        ),
        in_specs=[SMEM, SMEM, SMEM, VMEM],
        out_specs=(VMEM, VMEM, VMEM),
        compiler_params=params(),
        name="mask_and_pack",
    )(place, send, pno_count, amps_in)

    def exchange(packed):
        packed = packed.reshape(dev_count * aux_count, per_dev, rows, width)
        got = lax.all_to_all(packed, ("pairs", "aux"), split_axis=0, concat_axis=0, tiled=True)
        return got.reshape(dev_count, aux_count, per_dev, rows, width)

    amps_far = exchange(amps_out)
    block = 8
    by_pair = lambda *dims: pl.BlockSpec((block,) + dims, lambda step: (step,) + (0,) * len(dims))
    fit = fit_left.shape[2]
    wide = by_pair(width, width)
    slab = by_pair(rows, width)
    start, scale, own = pl.pallas_call(
        prepare_kernel,
        grid=(pair_dev // block,),
        out_shape=(
            shape((pair_dev, width, width), f32),
            shape(amps_in.shape, f32),
            shape(amps_in.shape, f32),
        ),
        in_specs=[SMEM, SMEM, SMEM, by_pair(width, fit), by_pair(width, fit), wide, slab, slab],
        out_specs=(wide, slab, slab),
        compiler_params=params(),
        cost_estimate=pl.CostEstimate(
            flops=2 * pair_dev * width * width * (fit + 2 * rows),
            bytes_accessed=2 * fit_left.size * 2 + pair_dev * width * width * 12,
            transcendentals=0,
        ),
        name="integrals",
    )(place, pno_count, energy, fit_left, fit_right, virt_fock, kept, half)

    items = (dev_count - 1) * per_dev
    projectors = pl.pallas_call(
        functools.partial(projector_kernel, slots),
        out_shape=shape((items, width, width), bf16),
        in_specs=[SMEM, SMEM] + [VMEM] * dev_count,
        out_specs=VMEM,
        compiler_params=params(),
        name="projectors",
    )(place, coef_read, pno_coef, *coef_far)

    def coupled(amps_far, start, scaled):
        if scaled:
            out = shape((aux_count, pair_dev + 1, rows, width), f32)
        else:
            out = shape((aux_count, pair_dev, rows, width), bf16)
        return pl.pallas_call(
            functools.partial(coupling_kernel, slots, all_slots, scaled),
            out_shape=(out, shape(amps_in.shape, f32), shape((pair_dev, width, width), f32)),
            in_specs=[SMEM, SMEM, SMEM, VMEM, VMEM, VMEM],
            out_specs=(VMEM, VMEM, VMEM),
            compiler_params=params(),
            name="coupling",
        )(place, read, weight, projectors, amps_far, start)

    to_sum, mine, part = coupled(amps_far, start, True)
    is_value = (jnp.arange(pair_dev + 1) < pair_dev)[None, :, None, None]
    power = to_sum[:, pair_dev:]
    to_sum = jnp.where(is_value, to_sum * jnp.exp2(-power), to_sum).astype(jnp.float16)
    got = lax.all_to_all(to_sum, "aux", split_axis=0, concat_axis=0, tiled=True)
    got = got.astype(f32)
    foreign = (jnp.arange(aux_count) != place[1])[:, None, None, None]
    got = jnp.where(foreign, got[:, :pair_dev] * jnp.exp2(got[:, pair_dev:]), 0.0)
    sums = mine + jnp.sum(got, axis=0)

    before = half
    kept, half, amps_out = pl.pallas_call(
        first_update_kernel,
        out_shape=(
            shape(amps_in.shape, f32),
            shape(amps_in.shape, bf16),
            shape((places, rows, width), bf16),
        ),
        in_specs=[SMEM] + [VMEM] * 4,
        out_specs=(VMEM,) * 3,
        compiler_params=params(),
        name="first_update",
    )(send, sums, own, scale, kept)

    amps_far = exchange(amps_out)

    start, own = pl.pallas_call(
        between_kernel,
        grid=(pair_dev // block,),
        out_shape=(shape((pair_dev, width, width), f32), shape(amps_in.shape, f32)),
        in_specs=[SMEM, SMEM, wide, slab, slab, slab, slab, wide],
        out_specs=(wide, slab),
        compiler_params=params(),
        cost_estimate=pl.CostEstimate(
            flops=6 * pair_dev * width * width * rows,
            bytes_accessed=pair_dev * width * width * 10,
            transcendentals=0,
        ),
        name="between",
    )(place, energy, virt_fock, kept, half, before, sums, part)

    to_sum, mine, _ = coupled(amps_far, start, False)
    got = lax.all_to_all(to_sum, "aux", split_axis=0, concat_axis=0, tiled=True)

    return pl.pallas_call(
        last_update_kernel,
        out_shape=shape(amps_in.shape, f32),
        in_specs=[SMEM] + [VMEM] * 5,
        out_specs=VMEM,
        compiler_params=params(),
        name="last_update",
    )(place, got, mine, own, scale, kept)


def solution(mesh):
    return jax.shard_map(
        per_device,
        mesh=mesh,
        in_specs=(
            P("pairs", None),
            P("pairs"),
            P("pairs", "aux"),
            P("pairs", "aux"),
            P("pairs", "aux"),
            P(),
            P("pairs", None, "aux"),
            P("pairs", None, "aux"),
            P("pairs", None, None),
            P("pairs", None, None),
            P("pairs", "aux", None),
        ),
        out_specs=P("pairs", "aux", None),
        check_vma=False,
    )
```

time: 479 us -> 274 us (0.57)
  local copies, waits for them, and re-layouts: 143 us -> 21.1 us
  waiting for transfers between devices: 195 us -> 103 us
  matrix products: 82.7 us -> 0.73 us
  Pallas kernels: 0 us -> 55.7 us
  blocking collectives: 0 us -> 53.7 us
  between operations: 13.6 us -> 0.45 us
  starting transfers between devices: 34.8 us -> 24.4 us
  other arithmetic: 6.82 us -> 12.7 us
    reduce_scatter x3 -> x0, waiting for transfers between devices: 134 us -> none  [the longest x2 134 us: per_device(): lax.psum_scatter(coupling, 'aux', scatter_dimension=1, tiled=True)]
    scatter x9 -> x0, local copies, waits for them, and re-layouts: 97.6 us -> none  [pack_slots(): filled = blank_buffer.at[send_place].set(values, mode='drop')]
    dot_general x14 -> x0, matrix products: 82.3 us -> none  [the longest x6 39.5 us: coupled_term(): jnp.einsum('pac,pdc->pad', mixed_amp, projector, preferred_element_type=j...]
    all_to_all x9 -> x3, waiting for transfers between devices: 14.2 us -> 74 us  [the longest x1 49.5 us: per_device(): got = lax.all_to_all(to_sum, 'aux', split_axis=0, concat_axis=0, tiled=True)]
    pallas_call x0 -> x9, Pallas kernels: none -> 55.7 us  [the longest x2 20.8 us: coupled(): pl.pallas_call(functools.partial(coupling_kernel, slots, all_slots, scale...]
    all_to_all x0 -> x1, blocking collectives: none -> 53.7 us  [per_device(): got = lax.all_to_all(to_sum, 'aux', split_axis=0, concat_axis=0, tiled=True)]
    all_gather x2 -> x0, waiting for transfers between devices: 46.6 us -> none  [per_device(): lax.all_gather(amps_rows.astype(jnp.bfloat16), 'aux', axis=1, tiled=True)]
    ppermute x0 -> x10, waiting for transfers between devices: none -> 29.2 us  [the longest x7 25.3 us: per_device(): lax.ppermute(coef_out[turn], 'pairs', [(dev, dev ^ turn + 1) for dev in r...]
  transfers between devices with their start and end apart: 14 -> 13, of which waited for: 8 -> 8; matrix products, arithmetic and copies ran while one was open for 41% -> 3% of each run, Pallas kernels for 0% -> 9%
where the time goes in v1:
time: 274 us; the launch traced here: 272 us
  waiting for transfers between devices  103 us (38%)
  Pallas kernels  55.7 us (20%)
  blocking collectives  53.7 us (20%)
  starting transfers between devices  24.4 us (9%)
  local copies, waits for them, and re-layouts  21.1 us (8%)
  other arithmetic  12.7 us (5%)
    all_to_all x1, blocking collectives, per_device(): got = lax.all_to_all(to_sum, 'aux', split_axis=0, concat_axis=0, tiled=True)  53.7 us
    all_to_all x1, waiting for transfers between devices, per_device(): got = lax.all_to_all(to_sum, 'aux', split_axis=0, concat_axis=0, tiled=True)  49.5 us
    ppermute x7, waiting for transfers between devices, per_device(): lax.ppermute(coef_out[turn], 'pairs', [(dev, dev ^ turn + 1) for dev in r...  25.3 us
    all_to_all x2, waiting for transfers between devices, exchange(): lax.all_to_all(packed, ('pairs', 'aux'), split_axis=0, concat_axis=0, til...  24.4 us
    pallas_call x2, Pallas kernels, coupled(): pl.pallas_call(functools.partial(coupling_kernel, slots, all_slots, scale...  20.8 us
    unnamed x60, local copies, waits for them, and re-layouts  14.5 us
    pallas_call x1, Pallas kernels, per_device(): pl.pallas_call(prepare_kernel, grid=(pair_dev // block,), out_shape=(shap...  12.4 us
    pallas_call x1, Pallas kernels, per_device(): pl.pallas_call(between_kernel, grid=(pair_dev // block,), out_shape=(shap...  8.18 us
  transfers between devices with their start and end apart: 13, of which 8 were waited for; matrix products, arithmetic and copies ran while one was open for 3% of the time, Pallas kernels for 9%

profile of v1, /device:TPU:0, one launch (start us, length us, event | category | flops | bytes accessed | tf_op | source)
XLA Modules:
  0.0 271.9 jit_solution(12559525998596495452)
XLA Ops:
  0.0 0.8 iota_add_fusion.1
  0.8 0.2 select_reduce_fusion.2
  0.9 0.3 fusion.11
  1.5 0.7 pad_add_fusion
  2.2 3.8 %pack_coef.1 = (bf16[6,256,128]{2,1,0:T(8,128)(2,1)S(1)}, bf16[6,256,128]{2,1,0:T(8,128)(2,1)S(1)}, bf16[6,256,128]{2,1,0:T(8,128)(2,1)S(1)}, bf16[6,256,128]{2,...) custom-call(s32[2]{0:T(128)S(1)} %pad_add_fusion.5.place_ref, ...), custom_call_target="tpu_custom_call" | custom-call | tf_op jit(solution)/shard_map/pack_coef/pallas_call | solution.py:289
  6.0 0.8 copy-done.24
  6.8 0.7 copy-done.25
  7.5 0.8 copy-done.26
  8.3 4.9 %collective-permute-start = (s32[64,9]{0,1:T(8,128)S(1)}, s32[64,9]{0,1:T(8,128)S(1)}, u32[]{:S(2)}, u32[]{:S(2)}) collective-permute-start(s32[64,9]{0,1:T(8,128)S(1)} %pad_add_fusion), channel_id=1, source_target_pairs={{0,3},{1,0},{2,1},{3,2},{4,7},{5,4},{6,5},{7,6},{8,11},{9,8},{10,9... | collective-permute-start | bytes 6920 | tf_op jit(solution)/shard_map/ppermute | solution.py:313
  13.3 1.2 collective-permute-start.2
  14.7 3.1 %collective-permute-done.1 = s32[64,9]{0,1:T(8,128)S(1)} collective-permute-done((s32[64,9]{0,1:T(8,128)S(1)}, s32[64,9]{0,1:T(8,128)S(1)}, u32[]{:S(2)}, u32[]{:S(2)}) %collective-permute-start.1) | collective-permute-done | bytes 2336 | tf_op jit(solution)/shard_map/ppermute | solution.py:313
  17.9 0.8 collective-permute-done.2
  18.9 0.3 select_select_fusion
  19.1 0.7 fusion.22
  20.0 0.5 fusion.9
  20.5 0.5 fusion.8
  21.2 0.1 copy.51
  21.5 1.2 copy-done.17
  22.7 1.1 mask_and_pack.1
  23.8 0.8 copy-done.9
  24.6 1.2 copy-done.12
  25.8 3.8 %all-to-all-start = ((bf16[32,6,32,128]{3,2,1,0:T(8,128)(2,1)}), bf16[32,6,32,128]{3,2,1,0:T(8,128)(2,1)}, u32[]{:S(2)}, u32[]{:S(2)}) async-start(bf16[32,6,32,128]{3,2,1,0:T(8,128)(2,1)} %bitcast.38), calls=%async_computation | async-start | bytes 3145728 | tf_op jit(solution)/shard_map/all_to_all | solution.py:355
  29.6 0.3 collective-permute-start.3
  29.9 1.7 collective-permute-start.4
  31.6 1.7 collective-permute-start.6
  33.6 2.3 gather_fusion
  36.0 0.2 select_reduce_fusion.energy_ref
  36.6 1.1 eq.176
  37.8 0.9 slice_compare_fusion
  38.7 0.2 eq.172
  39.0 0.7 fusion.3
  39.8 2.6 collective-permute-start.8
  42.4 12.7 %collective-permute-done.4.rest_1_ = bf16[6,256,128]{2,1,0:T(8,128)(2,1)} collective-permute-done((bf16[6,256,128]{2,1,0:T(8,128)(2,1)}, bf16[6,256,128]{2,1,0:T(8,128)(2,1)}, u32[]{:S(2)}, u32[]{:S(2)}) %collective-permute-start.4) | collective-permute-done | bytes 393248 | tf_op jit(solution)/shard_map/ppermute | solution.py:308
  55.1 0.1 copy.47
  55.2 0.1 reshape.160
  55.4 1.0 copy-done.10
  56.4 12.4 %integrals.1 = (f32[64,128,128]{2,1,0:T(8,128)}, f32[64,32,128]{2,1,0:T(8,128)S(1)}, f32[64,32,128]{2,1,0:T(8,128)S(1)}) custom-call(s32[2]{0:T(128)S(1)} %pad_add_fusion.5.place_ref, s32[64]{0:T(128)S(1)} %copy-done.20, f32[64]{0:T(128)S(1)} %select_reduce_fusion.energy_ref, bf16[64,128,512]{2,1,0:T(8,128)(2,1)} %left_ref.1, ...), custom_call_target="tpu_custom_call" | custom-call | flops 1207959552 | bytes 29360128 | tf_op jit(solution)/shard_map/integrals/pallas_call | solution.py:364
  68.8 1.0 copy-done.3
  69.8 1.0 copy-done.13
  70.8 5.2 %collective-permute-done.8.rest_5_ = bf16[6,256,128]{2,1,0:T(8,128)(2,1)} collective-permute-done((bf16[6,256,128]{2,1,0:T(8,128)(2,1)}, bf16[6,256,128]{2,1,0:T(8,128)(2,1)}, u32[]{:S(2)}, u32[]{:S(2)}) %collective-permute-start.8) | collective-permute-done | bytes 393248 | tf_op jit(solution)/shard_map/ppermute | solution.py:308
  76.0 7.5 %collective-permute-done.9.rest_6_ = bf16[6,256,128]{2,1,0:T(8,128)(2,1)} collective-permute-done((bf16[6,256,128]{2,1,0:T(8,128)(2,1)}, bf16[6,256,128]{2,1,0:T(8,128)(2,1)}, u32[]{:S(2)}, u32[]{:S(2)}) %collective-permute-start.9) | collective-permute-done | bytes 393248 | tf_op jit(solution)/shard_map/ppermute | solution.py:308
  83.5 3.9 %projectors.1.proj_ref = bf16[42,128,128]{2,1,0:T(8,128)(2,1)S(1)} custom-call(s32[2]{0:T(128)S(1)} %pad_add_fusion.5.place_ref, s32[48]{0:T(128)S(1)} %compare_select_fusion.10.read_ref, bf16[64,256,128]{2,1,0:T(8,128)(2,1)} %coef_ref.3, bf16[6,256,128]{2,1,0:T(8,128)(2,1)} %collective-permute-done.3.rest_0_, ...), custom_call_target="tpu_custom_call" | custom-call | tf_op jit(solution)/shard_map/projectors/pallas_call | solution.py:384
  87.4 11.0 %coupling.2 = (f32[4,65,32,128]{3,2,1,0:T(8,128)}, f32[64,32,128]{2,1,0:T(8,128)S(1)}, f32[64,128,128]{2,1,0:T(8,128)}) custom-call(s32[2]{0:T(128)S(1)} %pad_add_fusion.5.place_ref, s32[192]{0:T(256)S(1)} %compare_select_fusion.11.read_ref, f32[768]{0:T(1024)S(1)} %neg.6.weight_ref, bf16[42,128,128]{2,1,0:T(8,128)(2,1)S(1)} %projectors.1.proj_ref, ...), custom_call_target="tpu_custom_call" | custom-call | tf_op jit(solution)/shard_map/coupling/pallas_call | solution.py:398
  98.4 0.9 exponential_bitcast_fusion
  99.3 4.2 %fusion = f16[4,65,32,128]{3,2,1,0:T(8,128)(2,1)} fusion(f32[4,65,32,128]{3,2,1,0:T(8,128)} %get-tuple-element.56, f32[4,32,128]{2,1,0:T(8,128)S(1)} %exponential_bitcast_fusion, pred[65]{0:T(512)(128)(4,1)S(1)} %iota_compare_fusion.6), kind=kLoop, calls=%fused_computation.2 | loop fusion | flops 3194880 | bytes 6455361 | tf_op jit(solution)/shard_map/convert_element_type | solution.py:410
  103.6 4.6 %all-to-all-start.1 = ((f16[4,65,32,128]{3,2,1,0:T(8,128)(2,1)}), f16[4,65,32,128]{3,2,1,0:T(8,128)(2,1)}, u32[]{:S(2)}, u32[]{:S(2)}) async-start(f16[4,65,32,128]{3,2,1,0:T(8,128)(2,1)} %fusion), calls=%async_computation.1 | async-start | bytes 4259840 | tf_op jit(solution)/shard_map/all_to_all | solution.py:411
  108.2 49.5 %all-to-all-done.1 = f16[4,65,32,128]{3,2,1,0:T(8,128)(2,1)} async-done(((f16[4,65,32,128]{3,2,1,0:T(8,128)(2,1)}), f16[4,65,32,128]{3,2,1,0:T(8,128)(2,1)}, u32[]{:S(2)}, u32[]{:S(2)}) %all-to-all-start.1) | async-done | bytes 2129952 | tf_op jit(solution)/shard_map/all_to_all | solution.py:411
  157.8 2.2 convert_element_type.8
  160.0 0.7 fusion.2
  160.7 0.5 copy-done.16
  161.2 0.2 add.44.sum_ref
  161.5 0.3 copy-done.14
  161.8 2.4 first_update.1
  164.3 1.0 copy-done.6
  165.2 0.8 copy-done.18
  166.0 3.4 %all-to-all-start.2 = ((bf16[32,6,32,128]{3,2,1,0:T(8,128)(2,1)}), bf16[32,6,32,128]{3,2,1,0:T(8,128)(2,1)}, u32[]{:S(2)}, u32[]{:S(2)}) async-start(bf16[32,6,32,128]{3,2,1,0:T(8,128)(2,1)} %bitcast.40), calls=%async_computation.2 | async-start | bytes 3145728 | tf_op jit(solution)/shard_map/all_to_all | solution.py:355
  169.5 1.2 copy-done.7
  170.7 1.0 copy-done.11
  171.7 1.0 copy-done.19
  172.8 8.2 %between.1 = (f32[64,128,128]{2,1,0:T(8,128)}, f32[64,32,128]{2,1,0:T(8,128)S(1)}) custom-call(s32[2]{0:T(128)S(1)} %pad_add_fusion.5.place_ref, f32[64]{0:T(128)S(1)} %select_reduce_fusion.energy_ref, bf16[64,128,128]{2,1,0:T(8,128)(2,1)} %fock_ref.3, f32[64,32,128]{2,1,0:T(8,128)S(1)} %copy-done.7, bf16[64,32,128]{2,1,0:T(8,128)(2,1)S(1)} %copy-done.19, ...), custom_call_target="tpu_custom_call" | custom-call | flops 201326592 | bytes 10485760 | tf_op jit(solution)/shard_map/between/pallas_call | solution.py:433
  180.9 24.4 %all-to-all-done.2 = bf16[32,6,32,128]{3,2,1,0:T(8,128)(2,1)} async-done(((bf16[32,6,32,128]{3,2,1,0:T(8,128)(2,1)}), bf16[32,6,32,128]{3,2,1,0:T(8,128)(2,1)}, u32[]{:S(2)}, u32[]{:S(2)}) %all-to-all-start.2) | async-done | bytes 1572896 | tf_op jit(solution)/shard_map/all_to_all | solution.py:355
  205.4 9.7 %coupling.3 = (bf16[4,64,32,128]{3,2,1,0:T(8,128)(2,1)S(1)}, f32[64,32,128]{2,1,0:T(8,128)S(1)}, f32[64,128,128]{2,1,0:T(8,128)}) custom-call(s32[2]{0:T(128)S(1)} %pad_add_fusion.5.place_ref, s32[192]{0:T(256)S(1)} %compare_select_fusion.11.read_ref, f32[768]{0:T(1024)S(1)} %neg.6.weight_ref, bf16[42,128,128]{2,1,0:T(8,128)(2,1)S(1)} %projectors.1.proj_ref, ...), custom_call_target="tpu_custom_call" | custom-call | tf_op jit(solution)/shard_map/coupling/pallas_call | solution.py:398
  215.1 53.7 %all_to_all.20.got_ref = bf16[4,64,32,128]{3,2,1,0:T(8,128)(2,1)} all-to-all(bf16[4,64,32,128]{3,2,1,0:T(8,128)(2,1)S(1)} %get-tuple-element.64), channel_id=1, replica_groups=mesh['pairs'=8,'aux'=4] {'aux'}, dimensions={0} | all-to-all | bytes 4194304 | tf_op jit(solution)/shard_map/all_to_all | solution.py:449
  268.8 3.1 %last_update.1 = f32[64,32,128]{2,1,0:T(8,128)} custom-call(s32[2]{0:T(128)S(1)} %pad_add_fusion.5.place_ref, bf16[4,64,32,128]{3,2,1,0:T(8,128)(2,1)} %all_to_all.20.got_ref, f32[64,32,128]{2,1,0:T(8,128)S(1)} %get-tuple-element.65.mine_ref, f32[64,32,128]{2,1,0:T(8,128)S(1)} %get-tuple-element.66.own_ref, f32[64,32,128]{2,1,0:T(8,128)S(1)} %copy-done.5, ...), custom_call_target="tpu_custom_call" | custom-call | tf_op jit(solution)/shard_map/last_update/pallas_call | solution.py:451
  (96 shorter events, 2.4 us)
Async XLA Ops:
  0.0 33.6 %copy-start = (f32[256,256]{1,0:T(8,128)S(1)}, f32[256,256]{1,0:T(8,128)}, u32[]{:S(2)}) copy-start(f32[256,256]{1,0:T(8,128)} %param.16) | copy-start | bytes 786436
  0.0 21.5 %copy-start.20 = (s32[64]{0:T(128)S(1)}, s32[64]{0:T(128)}, u32[]{:S(2)}) copy-start(s32[64]{0:T(128)} %count_ref.3) | copy-start | bytes 772
  6.0 0.8 copy-start.24
  6.8 0.7 copy-start.25
  7.5 0.8 copy-start.26
  8.3 10.6 %copy-start.21 = (bf16[6,256,128]{2,1,0:T(8,128)(2,1)}, bf16[6,256,128]{2,1,0:T(8,128)(2,1)S(1)}, u32[]{:S(2)}) copy-start(bf16[6,256,128]{2,1,0:T(8,128)(2,1)S(1)} %get-tuple-element.50) | copy-start | bytes 1179652
  8.3 10.6 %copy-start.22 = (bf16[6,256,128]{2,1,0:T(8,128)(2,1)}, bf16[6,256,128]{2,1,0:T(8,128)(2,1)S(1)}, u32[]{:S(2)}) copy-start(bf16[6,256,128]{2,1,0:T(8,128)(2,1)S(1)} %get-tuple-element.49) | copy-start | bytes 1179652
  8.3 10.6 %copy-start.23 = (bf16[6,256,128]{2,1,0:T(8,128)(2,1)}, bf16[6,256,128]{2,1,0:T(8,128)(2,1)S(1)}, u32[]{:S(2)}) copy-start(bf16[6,256,128]{2,1,0:T(8,128)(2,1)S(1)} %get-tuple-element.48) | copy-start | bytes 1179652
  8.3 13.2 %copy-start.27 = (bf16[6,256,128]{2,1,0:T(8,128)(2,1)}, bf16[6,256,128]{2,1,0:T(8,128)(2,1)S(1)}, u32[]{:S(2)}) copy-start(bf16[6,256,128]{2,1,0:T(8,128)(2,1)S(1)} %get-tuple-element.44) | copy-start | bytes 1179652
  8.3 27.7 %copy-start.29 = (s32[64,2]{0,1:T(2,128)S(1)}, s32[64,2]{0,1:T(2,128)}, u32[]{:S(2)}) copy-start(s32[64,2]{0,1:T(2,128)} %param.11) | copy-start | bytes 1540
  8.3 6.3 %collective-permute-start = (s32[64,9]{0,1:T(8,128)S(1)}, s32[64,9]{0,1:T(8,128)S(1)}, u32[]{:S(2)}, u32[]{:S(2)}) collective-permute-start(s32[64,9]{0,1:T(8,128)S(1)} %pad_add_fusion), channel_id=1, source_target_pairs={{0,3},{1,0},{2,1},{3,2},{4,7},{5,4},{6,5},{7,6},{8,11},{9,8},{10,9... | collective-permute-start | bytes 6920 | tf_op jit(solution)/shard_map/ppermute | solution.py:313
  13.3 4.5 %collective-permute-start.1 = (s32[64,9]{0,1:T(8,128)S(1)}, s32[64,9]{0,1:T(8,128)S(1)}, u32[]{:S(2)}, u32[]{:S(2)}) collective-permute-start(s32[64,9]{0,1:T(8,128)S(1)} %pad_add_fusion), channel_id=1, source_target_pairs={{0,2},{1,3},{2,0},{3,1},{4,6},{5,7},{6,4},{7,5},{8,10},{9,11},{10,... | collective-permute-start | bytes 6920 | tf_op jit(solution)/shard_map/ppermute | solution.py:313
  13.3 5.4 %collective-permute-start.2 = (s32[64,9]{0,1:T(8,128)S(1)}, s32[64,9]{0,1:T(8,128)S(1)}, u32[]{:S(2)}, u32[]{:S(2)}) collective-permute-start(s32[64,9]{0,1:T(8,128)S(1)} %pad_add_fusion), channel_id=1, source_target_pairs={{0,1},{1,2},{2,3},{3,0},{4,5},{5,6},{6,7},{7,4},{8,9},{9,10},{10,1... | collective-permute-start | bytes 6920 | tf_op jit(solution)/shard_map/ppermute | solution.py:313
  19.1 2.3 copy-start.28
  19.1 36.2 %copy-start.2 = (bf16[64,128,128]{2,1,0:T(8,128)(2,1)S(1)}, bf16[64,128,128]{2,1,0:T(8,128)(2,1)}, u32[]{:S(2)}) copy-start(bf16[64,128,128]{2,1,0:T(8,128)(2,1)} %fock_ref.3) | copy-start | bytes 6291460
  21.5 1.2 copy-start.17
  23.8 0.8 copy-start.9
  24.6 1.2 copy-start.12
  25.8 61.6 %all-to-all-start = ((bf16[32,6,32,128]{3,2,1,0:T(8,128)(2,1)}), bf16[32,6,32,128]{3,2,1,0:T(8,128)(2,1)}, u32[]{:S(2)}, u32[]{:S(2)}) async-start(bf16[32,6,32,128]{3,2,1,0:T(8,128)(2,1)} %bitcast.38), calls=%async_computation | async-start | bytes 3145728 | tf_op jit(solution)/shard_map/all_to_all | solution.py:355
  29.6 10.1 %collective-permute-start.3 = (bf16[6,256,128]{2,1,0:T(8,128)(2,1)}, bf16[6,256,128]{2,1,0:T(8,128)(2,1)}, u32[]{:S(2)}, u32[]{:S(2)}) collective-permute-start(bf16[6,256,128]{2,1,0:T(8,128)(2,1)} %copy-done.27), channel_id=1, source_target_pairs={{0,4},{4,0},{8,12},{12,8},{16,20},{20,16},{24,28},{28,24},{1,5},{5... | collective-permute-start | bytes 1179656 | tf_op jit(solution)/shard_map/ppermute | solution.py:308
  29.9 25.2 %collective-permute-start.4 = (bf16[6,256,128]{2,1,0:T(8,128)(2,1)}, bf16[6,256,128]{2,1,0:T(8,128)(2,1)}, u32[]{:S(2)}, u32[]{:S(2)}) collective-permute-start(bf16[6,256,128]{2,1,0:T(8,128)(2,1)} %copy-done.26), channel_id=1, source_target_pairs={{0,8},{4,12},{8,0},{12,4},{16,24},{20,28},{24,16},{28,20},{1,9},{5... | collective-permute-start | bytes 1179656 | tf_op jit(solution)/shard_map/ppermute | solution.py:308
  31.6 39.3 %collective-permute-start.5 = (bf16[6,256,128]{2,1,0:T(8,128)(2,1)}, bf16[6,256,128]{2,1,0:T(8,128)(2,1)}, u32[]{:S(2)}, u32[]{:S(2)}) collective-permute-start(bf16[6,256,128]{2,1,0:T(8,128)(2,1)} %copy-done.25), channel_id=1, source_target_pairs={{0,12},{4,8},{8,4},{12,0},{16,28},{20,24},{24,20},{28,16},{1,13},{... | collective-permute-start | bytes 1179656 | tf_op jit(solution)/shard_map/ppermute | solution.py:308
  31.6 39.2 %collective-permute-start.6 = (bf16[6,256,128]{2,1,0:T(8,128)(2,1)}, bf16[6,256,128]{2,1,0:T(8,128)(2,1)}, u32[]{:S(2)}, u32[]{:S(2)}) collective-permute-start(bf16[6,256,128]{2,1,0:T(8,128)(2,1)} %copy-done.24), channel_id=1, source_target_pairs={{0,16},{4,20},{8,24},{12,28},{16,0},{20,4},{24,8},{28,12},{1,17},{... | collective-permute-start | bytes 1179656 | tf_op jit(solution)/shard_map/ppermute | solution.py:308
  33.3 37.6 %collective-permute-start.7 = (bf16[6,256,128]{2,1,0:T(8,128)(2,1)}, bf16[6,256,128]{2,1,0:T(8,128)(2,1)}, u32[]{:S(2)}, u32[]{:S(2)}) collective-permute-start(bf16[6,256,128]{2,1,0:T(8,128)(2,1)} %copy-done.23), channel_id=1, source_target_pairs={{0,20},{4,16},{8,28},{12,24},{16,4},{20,0},{24,12},{28,8},{1,21},{... | collective-permute-start | bytes 1179656 | tf_op jit(solution)/shard_map/ppermute | solution.py:308
  39.8 36.2 %collective-permute-start.8 = (bf16[6,256,128]{2,1,0:T(8,128)(2,1)}, bf16[6,256,128]{2,1,0:T(8,128)(2,1)}, u32[]{:S(2)}, u32[]{:S(2)}) collective-permute-start(bf16[6,256,128]{2,1,0:T(8,128)(2,1)} %copy-done.22), channel_id=1, source_target_pairs={{0,24},{4,28},{8,16},{12,20},{16,8},{20,12},{24,0},{28,4},{1,25},{... | collective-permute-start | bytes 1179656 | tf_op jit(solution)/shard_map/ppermute | solution.py:308
  55.1 28.4 %collective-permute-start.9 = (bf16[6,256,128]{2,1,0:T(8,128)(2,1)}, bf16[6,256,128]{2,1,0:T(8,128)(2,1)}, u32[]{:S(2)}, u32[]{:S(2)}) collective-permute-start(bf16[6,256,128]{2,1,0:T(8,128)(2,1)} %copy-done.21), channel_id=1, source_target_pairs={{0,28},{4,24},{8,20},{12,16},{16,12},{20,8},{24,4},{28,0},{1,29},{... | collective-permute-start | bytes 1179656 | tf_op jit(solution)/shard_map/ppermute | solution.py:308
  55.4 1.0 copy-start.10
  68.8 1.0 copy-start.3
  69.8 1.0 copy-start.13
  98.4 5.1 %copy-start.15 = (f32[64,32,128]{2,1,0:T(8,128)}, f32[64,32,128]{2,1,0:T(8,128)S(1)}, u32[]{:S(2)}) copy-start(f32[64,32,128]{2,1,0:T(8,128)S(1)} %get-tuple-element.55) | copy-start | bytes 3145732
  103.6 54.2 %all-to-all-start.1 = ((f16[4,65,32,128]{3,2,1,0:T(8,128)(2,1)}), f16[4,65,32,128]{3,2,1,0:T(8,128)(2,1)}, u32[]{:S(2)}, u32[]{:S(2)}) async-start(f16[4,65,32,128]{3,2,1,0:T(8,128)(2,1)} %fusion), calls=%async_computation.1 | async-start | bytes 4259840 | tf_op jit(solution)/shard_map/all_to_all | solution.py:411
  159.9 1.2 copy-start.16
  160.0 1.5 copy-start.4
  160.0 1.8 copy-start.14
  164.3 1.0 copy-start.6
  165.2 0.8 copy-start.18
  166.0 39.3 %all-to-all-start.2 = ((bf16[32,6,32,128]{3,2,1,0:T(8,128)(2,1)}), bf16[32,6,32,128]{3,2,1,0:T(8,128)(2,1)}, u32[]{:S(2)}, u32[]{:S(2)}) async-start(bf16[32,6,32,128]{3,2,1,0:T(8,128)(2,1)} %bitcast.40), calls=%async_computation.2 | async-start | bytes 3145728 | tf_op jit(solution)/shard_map/all_to_all | solution.py:355
  169.4 1.2 copy-start.7
  170.7 1.0 copy-start.11
  171.7 1.0 copy-start.19
  205.4 63.5 %copy-start.5 = (f32[64,32,128]{2,1,0:T(8,128)S(1)}, f32[64,32,128]{2,1,0:T(8,128)}, u32[]{:S(2)}) copy-start(f32[64,32,128]{2,1,0:T(8,128)} %copy-done.3) | copy-start | bytes 3145732
  205.4 63.5 %copy-start.8 = (f32[64,32,128]{2,1,0:T(8,128)S(1)}, f32[64,32,128]{2,1,0:T(8,128)}, u32[]{:S(2)}) copy-start(f32[64,32,128]{2,1,0:T(8,128)} %copy-done.6) | copy-start | bytes 3145732
  215.1 56.8 %copy-start.1 = (f32[256,256]{1,0:T(8,128)S(1)}, f32[256,256]{1,0:T(8,128)}, u32[]{:S(2)}) copy-start(f32[256,256]{1,0:T(8,128)} %param.16) | copy-start | bytes 786436

commit v2 on v1

v2 whole, which is shorter than its diff:
```python
import functools

import jax
import jax.numpy as jnp
from jax import lax
from jax.experimental import pallas as pl
from jax.experimental.pallas import tpu as pltpu
from jax.sharding import PartitionSpec as P

MOST = 2
SPARE_BYTES = 3 * 1024 * 1024
WIDE_BYTES = 48 * 1024 * 1024

SMEM = pl.BlockSpec(memory_space=pltpu.SMEM)
VMEM = pl.BlockSpec(memory_space=pltpu.VMEM)
HBM = pl.BlockSpec(memory_space=pltpu.HBM)
FREE = pl.CostEstimate(flops=0, bytes_accessed=0, transcendentals=0)


def dot(left, right, over_left, over_right):
    return lax.dot_general(
        left, right, (((over_left,), (over_right,)), ((), ())), preferred_element_type=jnp.float32
    )


def params(*arrays):
    held = sum(array.size * array.dtype.itemsize for array in arrays)
    needed = held + held // 8 + SPARE_BYTES
    return pltpu.CompilerParams(vmem_limit_bytes=max(needed, WIDE_BYTES))


def pair_places(partner, pair_dev, dev_count, arrival):
    slots = partner.shape[1]
    owner = jnp.where(partner >= 0, partner // pair_dev, -1)
    own_id = jnp.broadcast_to(jnp.arange(pair_dev, dtype=jnp.int32)[:, None], partner.shape)
    far_key = (partner - owner * pair_dev) * pair_dev + own_id
    none = pair_dev * pair_dev
    devs = jnp.arange(dev_count, dtype=jnp.int32)[None, :, None]
    hit = owner[:, None, :] == devs

    def ranked(key):
        left = jnp.where(hit, key[:, None, :], none)
        found = []
        for _ in range(MOST):
            least = jnp.min(left, axis=0)
            found.append(least)
            left = jnp.where(left == least[None], none, left)
        return jnp.stack(found, axis=-1).reshape(-1)

    send = ranked(own_id)
    send = jnp.where(send < none, send, 0)
    if not arrival:
        return send
    read = ranked(far_key)
    return send, jnp.where(read < none, lax.rem(read, pair_dev), -1)


def pack_rows(send_ref, half_ref, out_ref, held, sems):
    chunk = held.shape[0] // sems.shape[0]

    def store(turn):
        at = pl.ds(pl.multiple_of(turn * chunk, chunk), chunk)
        return pltpu.make_async_copy(held.at[at], out_ref.at[at], sems.at[turn])

    def body(turn, carry):
        for item in range(chunk):
            place = turn * chunk + item
            held[place] = half_ref[send_ref[place]]
        store(turn).start()
        return carry

    def finish(turn, carry):
        store(turn).wait()
        return carry

    lax.fori_loop(0, sems.shape[0], body, 0)
    lax.fori_loop(0, sems.shape[0], finish, 0)


def start_kernel(
    place_ref, send_ref, count_ref, amps_ref, kept_ref, half_ref, out_ref, held, sems
):
    pairs, rows, width = amps_ref.shape
    row_id = lax.broadcasted_iota(jnp.int32, (rows, width), 0) + place_ref[1] * rows
    col_id = lax.broadcasted_iota(jnp.int32, (rows, width), 1)
    last = jnp.maximum(row_id, col_id)

    def body(pair, carry):
        kept = jnp.where(last < count_ref[pair], amps_ref[pair], 0.0)
        kept_ref[pair] = kept
        half_ref[pair] = kept.astype(jnp.bfloat16)
        return carry

    lax.fori_loop(0, pairs, body, 0, unroll=4)
    pack_rows(send_ref, half_ref, out_ref, held, sems)


def coef_kernel(slots, place_ref, send_ref, coef_ref, *rest):
    outs, (held, in_sems, out_sems) = rest[:-3], rest[-3:]
    per_dev = slots * MOST

    def fetch(turn, item):
        far = place_ref[0] ^ (turn + 1)
        pair = send_ref[far * per_dev + item]
        place = turn * per_dev + item
        return pltpu.make_async_copy(coef_ref.at[pair], held.at[place], in_sems.at[place])

    def store(turn):
        return pltpu.make_async_copy(
            held.at[pl.ds(turn * per_dev, per_dev)], outs[turn], out_sems.at[turn]
        )

    for turn in range(len(outs)):
        for item in range(per_dev):
            fetch(turn, item).start()
    for turn in range(len(outs)):
        for item in range(per_dev):
            fetch(turn, item).wait()
        store(turn).start()
    for turn in range(len(outs)):
        store(turn).wait()


def put_rows(out_ref, pair, value):
    rows = out_ref.shape[2]
    for part in range(out_ref.shape[0]):
        out_ref[part, pair] = value[part * rows : (part + 1) * rows]


def element(matrix_ref, row, column):
    line = matrix_ref[pl.ds(row, 1), :]
    at = lax.broadcasted_iota(jnp.int32, line.shape, 1) == column
    return jnp.sum(jnp.where(at, line, 0.0), axis=1, keepdims=True)


def left_part(fock_rows, half_rows):
    return dot(fock_rows, half_rows, 0, 0)


def prepare_kernel(
    place_ref, count_ref, orbit_ref, occ_ref, left_ref, right_ref, fock_ref, kept_ref, half_ref,
    part_ref, scale_ref, own_ref, energy_ref,
):
    block, rows, width = kept_ref.shape
    first = pl.program_id(0) * block
    row_start = pl.multiple_of(place_ref[1] * rows, rows)
    row_id = lax.broadcasted_iota(jnp.int32, (rows, width), 0) + row_start
    col_id = lax.broadcasted_iota(jnp.int32, (rows, width), 1)
    last = jnp.maximum(row_id, col_id)
    eye_rows = row_id == col_id
    eye = lax.broadcasted_iota(jnp.int32, (width, width), 0) == lax.broadcasted_iota(
        jnp.int32, (width, width), 1
    )
    for pair in range(block):
        at = orbit_ref.shape[0] - 2 * (count_ref.shape[0] - first - pair)
        orbit, other = orbit_ref[at], orbit_ref[at + 1]
        energy = element(occ_ref, orbit, orbit) + element(occ_ref, other, other)
        energy_ref[pair] = jnp.broadcast_to(energy, (1, width))
        fock = fock_ref[pair]
        fock_rows = fock_ref[pair, pl.ds(row_start, rows), :]
        half = half_ref[pair]
        fitted = dot(left_ref[pair], right_ref[pair], 1, 1)
        put_rows(part_ref, pair, fitted + left_part(fock_rows, half))
        own_ref[pair] = dot(half, fock, 1, 0) - energy * kept_ref[pair]
        diag_cols = jnp.sum(jnp.where(eye, fock.astype(jnp.float32), 0.0), axis=0, keepdims=True)
        diag_rows = jnp.sum(
            jnp.where(eye_rows, fock_rows.astype(jnp.float32), 0.0), axis=1, keepdims=True
        )
        denominator = diag_rows + diag_cols - energy
        scale_ref[pair] = jnp.where(last < count_ref[first + pair], 1.0 / denominator, 0.0)


def any_live(read_ref, first, per_dev, rank):
    most = read_ref[first + rank]
    for item in range(rank + MOST, per_dev, MOST):
        most = jnp.maximum(most, read_ref[first + item])
    return most >= 0


def own_coef_kernel(slots, place_ref, read_ref, coef_ref, out_ref):
    per_dev = slots * MOST

    def body(turn, carry):
        far = place_ref[0] ^ (turn + 1)
        for item in range(per_dev):
            pair = jnp.maximum(read_ref[far * per_dev + item], 0)
            out_ref[turn * per_dev + item] = coef_ref[pair].T
        return carry

    lax.fori_loop(0, out_ref.shape[0] // per_dev, body, 0)


def projector_kernel(turns, place_ref, read_ref, own_ref, *rest):
    arrived, out_ref = rest[:-1], rest[-1]
    per_dev = arrived[0].shape[0]

    def rank_items(place, turn, rank):
        for item in range(rank, per_dev, MOST):
            own = own_ref[turn * per_dev + item]
            out_ref[place * per_dev + item] = dot(own, arrived[place][item], 1, 0).astype(
                jnp.bfloat16
            )

    for place, turn in enumerate(turns):
        far = place_ref[0] ^ (turn + 1)
        for rank in range(MOST):
            pl.when(any_live(read_ref, far * per_dev, per_dev, rank))(
                functools.partial(rank_items, place, turn, rank)
            )


def add_coupling(
    groups, place_ref, read_ref, orbit_ref, occ_ref, proj_refs, fetch, amps_ref, part_ref
):
    per_dev = amps_ref.shape[2]
    slots = per_dev // MOST
    parts, pairs, rows = part_ref.shape[0], orbit_ref.shape[0] // (2 * slots + 2), part_ref.shape[2]
    side_at, pair_at = pairs * slots, 2 * pairs * slots

    def body(turn, place, proj_ref):
        width = proj_ref.shape[-1]
        far = place_ref[0] ^ (turn + 1)
        fetch(turn).wait()

        def rank_terms(rank):
            terms = []
            for item in range(rank, per_dev, MOST):
                pair = read_ref[far * per_dev + item]
                safe = jnp.maximum(pair, 0)
                entry = safe * slots + item // MOST
                orbit = orbit_ref[pair_at + 2 * safe + orbit_ref[side_at + entry]]
                coupled = element(occ_ref, orbit_ref[entry], orbit)
                weight = jnp.where(pair >= 0, -coupled, 0.0)
                proj = proj_ref[place * per_dev + item]
                amps = amps_ref[far, :, item].reshape(width, width)
                mixed = dot(proj, amps, 1, 0).astype(jnp.bfloat16)
                terms.append((safe, weight * dot(mixed, proj, 1, 1)))
            for safe, term in terms:
                for part in range(parts):
                    part_ref[part, safe] += term[part * rows : (part + 1) * rows]

        for rank in range(MOST):
            pl.when(any_live(read_ref, far * per_dev, per_dev, rank))(
                functools.partial(rank_terms, rank)
            )

    for turns, proj_ref in zip(groups, proj_refs):
        def step(place, carry, turns=turns, proj_ref=proj_ref):
            later = turns[min(1, len(turns) - 1)] - min(1, len(turns) - 1)
            body(jnp.where(place == 0, turns[0], place + later), place, proj_ref)
            return carry

        lax.fori_loop(0, len(turns), step, 0)


def coupling_kernel(
    groups, scaled, place_ref, read_ref, orbit_ref, occ_ref, early_ref, late_ref, amps_hbm,
    start_hbm, out_ref, extra_ref, amps_ref, amps_sems, start_sem, *rest,
):
    part_ref = out_ref if scaled else rest[0]
    parts, pairs, rows, width = start_hbm.shape

    def fetch(turn):
        far = place_ref[0] ^ (turn + 1)
        return pltpu.make_async_copy(amps_hbm.at[far], amps_ref.at[far], amps_sems.at[turn])

    loads = [
        pltpu.make_async_copy(
            start_hbm.at[part], part_ref.at[part, pl.ds(0, pairs)], start_sem.at[part]
        )
        for part in range(parts)
    ]
    for load in loads:
        load.start()
    for turns in groups:
        for turn in turns:
            fetch(turn).start()
    for load in loads:
        load.wait()
    add_coupling(
        groups, place_ref, read_ref, orbit_ref, occ_ref, (early_ref, late_ref), fetch, amps_ref,
        part_ref,
    )
    if not scaled:

        def body(pair, carry):
            for part in range(parts):
                out_ref[part, pair] = part_ref[part, pair].astype(out_ref.dtype)
            extra_ref[pair] = part_ref[place_ref[1], pair]
            return carry

        lax.fori_loop(0, pairs, body, 0, unroll=4)
        return

    def body(pair, most):
        for part in range(parts):
            most = jnp.maximum(most, jnp.abs(part_ref[part, pair]))
        return most

    most = lax.fori_loop(0, pairs, body, jnp.zeros((rows, width), jnp.float32), unroll=4)
    most = jnp.max(jnp.max(most, axis=0, keepdims=True), axis=1, keepdims=True)
    power = jnp.maximum(jnp.ceil(jnp.log2(jnp.maximum(most, 1.0)) - 15.0), 0.0)
    for part in range(parts):
        out_ref[part, pairs] = jnp.broadcast_to(power * jnp.exp2(power), (rows, width))
    extra_ref[...] = jnp.broadcast_to(jnp.exp2(-power), (1, width))


def first_update_kernel(
    send_ref, sum_ref, own_ref, scale_ref, kept_ref, new_ref, half_ref, out_ref, held, sems
):
    def body(pair, carry):
        new = kept_ref[pair] - (sum_ref[pair] + own_ref[pair]) * scale_ref[pair]
        new_ref[pair] = new
        half_ref[pair] = new.astype(jnp.bfloat16)
        return carry

    lax.fori_loop(0, new_ref.shape[0], body, 0, unroll=4)
    pack_rows(send_ref, half_ref, out_ref, held, sems)


def between_kernel(
    place_ref, energy_ref, fock_ref, kept_ref, half_ref, before_ref, sum_ref, start_ref, old_ref,
    part_ref, own_ref,
):
    block, rows, width = kept_ref.shape
    row_start = pl.multiple_of(place_ref[1] * rows, rows)
    for pair in range(block):
        half = half_ref[pair]
        fock_rows = fock_ref[pair, pl.ds(row_start, rows), :]
        change = left_part(fock_rows, half) - left_part(fock_rows, before_ref[pair])
        for part in range(part_ref.shape[0]):
            part_ref[part, pair] = (
                start_ref[part, pair] - old_ref[part, pair] + change[part * rows : (part + 1) * rows]
            )
        own_ref[pair] = (
            dot(half, fock_ref[pair], 1, 0)
            - energy_ref[pair] * kept_ref[pair]
            + sum_ref[pair]
        )


def last_update_kernel(place_ref, got_ref, mine_ref, own_ref, scale_ref, kept_ref, new_ref):
    def body(pair, carry):
        total = mine_ref[pair]
        for turn in range(1, got_ref.shape[0]):
            part = lax.rem(place_ref[1] + turn, got_ref.shape[0])
            total = total + got_ref[part, pair].astype(jnp.float32)
        new_ref[pair] = kept_ref[pair] - (total + own_ref[pair]) * scale_ref[pair]
        return carry

    lax.fori_loop(0, new_ref.shape[0], body, 0, unroll=4)


def shape(dims, dtype):
    return jax.ShapeDtypeStruct(tuple(dims), dtype)


def per_device(
    pair_orbits,
    pno_count,
    partner,
    couple_orbit,
    couple_side,
    occ_fock,
    fit_left,
    fit_right,
    pno_coef,
    virt_fock,
    amps_in,
):
    pair_dev = pno_count.shape[0]
    width = virt_fock.shape[1]
    rows = amps_in.shape[1]
    slots = partner.shape[1]
    dev_count = lax.axis_size("pairs")
    aux_count = lax.axis_size("aux")
    all_slots = slots * aux_count
    per_dev = slots * MOST
    items = (dev_count - 1) * per_dev
    bf16, f32 = jnp.bfloat16, jnp.float32
    place = jnp.stack([lax.axis_index("pairs"), lax.axis_index("aux")]).astype(jnp.int32)

    orbits = [couple_orbit.reshape(-1), couple_side.reshape(-1), pair_orbits.reshape(-1)]
    orbits = jnp.concatenate(orbits)
    coef_send, coef_read = pair_places(partner, pair_dev, dev_count, True)

    coef_out = pl.pallas_call(
        functools.partial(coef_kernel, slots),
        out_shape=tuple(
            shape((per_dev,) + pno_coef.shape[1:], bf16) for _ in range(dev_count - 1)
        ),
        in_specs=[SMEM, SMEM, HBM],
        out_specs=tuple(HBM for _ in range(dev_count - 1)),
        scratch_shapes=[
            pltpu.VMEM(((dev_count - 1) * per_dev,) + pno_coef.shape[1:], bf16),
            pltpu.SemaphoreType.DMA(((dev_count - 1) * per_dev,)),
            pltpu.SemaphoreType.DMA((dev_count - 1,)),
        ],
        compiler_params=params(shape((items,) + pno_coef.shape[1:], bf16)),
        cost_estimate=FREE,
        name="pack_coef",
    )(place, coef_send, pno_coef)

    tables = partner
    tables, coef_out = lax.optimization_barrier((tables, coef_out))
    coef_far = [
        lax.ppermute(coef_out[turn], "pairs", [(dev, dev ^ (turn + 1)) for dev in range(dev_count)])
        for turn in range(dev_count - 1)
    ]

    shares = [tables] + [
        lax.ppermute(tables, "aux", [(dev, (dev + turn) % aux_count) for dev in range(aux_count)])
        for turn in range(1, aux_count)
    ]
    tables = jnp.zeros((aux_count,) + tables.shape, jnp.int32)
    owners = jnp.arange(aux_count)[:, None, None]
    for turn, share in enumerate(shares):
        owner = lax.rem(place[1] + aux_count - turn, aux_count)
        tables = jnp.where(owners == owner, share[None], tables)
    tables = tables.transpose(1, 0, 2).reshape(pair_dev, all_slots)
    send = pair_places(tables, pair_dev, dev_count, False)

    places = dev_count * all_slots * MOST
    packed = shape((places, rows, width), bf16)
    pack_scratch = [pltpu.VMEM(packed.shape, bf16), pltpu.SemaphoreType.DMA((dev_count,))]
    kept, half, amps_out = pl.pallas_call(
        start_kernel,
        out_shape=(
            shape(amps_in.shape, f32),
            shape(amps_in.shape, bf16),
            packed,
        ),
        in_specs=[SMEM, SMEM, SMEM, VMEM],
        out_specs=(VMEM, VMEM, HBM),
        scratch_shapes=pack_scratch,
        compiler_params=params(amps_in, amps_in, amps_in, packed),
        cost_estimate=FREE,
        name="mask_and_pack",
    )(place, send, pno_count, amps_in)

    def exchange(packed):
        packed = packed.reshape(dev_count * aux_count, per_dev, rows, width)
        got = lax.all_to_all(packed, ("pairs", "aux"), split_axis=0, concat_axis=0, tiled=True)
        return got.reshape(dev_count, aux_count, per_dev, rows, width)

    ahead = slice(1, dev_count // 2 + 1)
    amps_out, coef_far[ahead] = lax.optimization_barrier((amps_out, coef_far[ahead]))
    amps_far = exchange(amps_out)

    block = 8
    by_pair = lambda *dims: pl.BlockSpec((block,) + dims, lambda step: (step,) + (0,) * len(dims))
    fit = fit_left.shape[2]
    wide = by_pair(width, width)
    slab = by_pair(rows, width)
    line = by_pair(1, width)
    tall = pl.BlockSpec((aux_count, block, rows, width), lambda step: (0, step, 0, 0))
    by_rows = shape((aux_count, pair_dev, rows, width), f32)
    start, scale, own, energy = pl.pallas_call(
        prepare_kernel,
        grid=(pair_dev // block,),
        out_shape=(
            by_rows,
            shape(amps_in.shape, f32),
            shape(amps_in.shape, f32),
            shape((pair_dev, 1, width), f32),
        ),
        in_specs=[SMEM, SMEM, SMEM, VMEM, by_pair(width, fit), by_pair(width, fit), wide, slab, slab],
        out_specs=(tall, slab, slab, line),
        compiler_params=pltpu.CompilerParams(vmem_limit_bytes=WIDE_BYTES),
        cost_estimate=FREE,
        name="integrals",
    )(place, pno_count, orbits, occ_fock, fit_left, fit_right, virt_fock, kept, half)

    own_shape = shape((items, width, pno_coef.shape[1]), bf16)
    own_coef = pl.pallas_call(
        functools.partial(own_coef_kernel, slots),
        out_shape=own_shape,
        in_specs=[SMEM, SMEM, VMEM],
        out_specs=VMEM,
        compiler_params=params(pno_coef, own_shape),
        name="own_coef",
    )(place, coef_read, pno_coef)

    early = tuple(range(dev_count - 1)[ahead])
    groups = (early, tuple(turn for turn in range(dev_count - 1) if turn not in early))
    projectors = []
    for turns in groups:
        arrived = [coef_far[turn] for turn in turns]
        out = shape((len(turns) * per_dev, width, width), bf16)
        projectors.append(
            pl.pallas_call(
                functools.partial(projector_kernel, turns),
                out_shape=out,
                in_specs=[SMEM, SMEM] + [VMEM] * (1 + len(turns)),
                out_specs=VMEM,
                compiler_params=params(own_coef, out, *arrived),
                name="projectors",
            )(place, coef_read, own_coef, *arrived)
        )

    def coupled(amps_far, start, scaled):
        if scaled:
            out, extra = shape((aux_count, pair_dev + 1, rows, width), f32), shape((1, width), f32)
        else:
            out, extra = shape(start.shape, bf16), shape(amps_in.shape, f32)
        return pl.pallas_call(
            functools.partial(coupling_kernel, groups, scaled),
            out_shape=(out, extra),
            in_specs=[SMEM] * 3 + [VMEM] * 3 + [HBM] * 2,
            out_specs=(VMEM, VMEM),
            scratch_shapes=[
                pltpu.VMEM(amps_far.shape, bf16),
                pltpu.SemaphoreType.DMA((dev_count - 1,)),
                pltpu.SemaphoreType.DMA((aux_count,)),
            ]
            + ([] if scaled else [pltpu.VMEM(start.shape, f32)]),
            compiler_params=params(out, amps_in, start, amps_far, *projectors),
            name="coupling",
        )(place, coef_read, orbits, occ_fock, *projectors, amps_far, start)

    total, shrink = coupled(amps_far, start, True)
    to_sum = (total * shrink).astype(jnp.float16)
    got = lax.all_to_all(to_sum, "aux", split_axis=0, concat_axis=0, tiled=True)
    foreign = (jnp.arange(aux_count) != place[1])[:, None, None, None]
    grow = jnp.where(foreign, jnp.exp2(got[:, pair_dev:, :1].astype(f32)), 0.0)
    sums = lax.dynamic_index_in_dim(total, place[1], 0, keepdims=False)[:pair_dev]
    for turn in range(aux_count):
        sums = sums + got[turn, :pair_dev].astype(f32) * grow[turn]

    before = half
    kept, half, amps_out = pl.pallas_call(
        first_update_kernel,
        out_shape=(
            shape(amps_in.shape, f32),
            shape(amps_in.shape, bf16),
            packed,
        ),
        in_specs=[SMEM] + [VMEM] * 4,
        out_specs=(VMEM, VMEM, HBM),
        scratch_shapes=pack_scratch,
        compiler_params=params(amps_in, amps_in, amps_in, amps_in, amps_in, amps_in, packed),
        name="first_update",
    )(send, sums, own, scale, kept)

    amps_far = exchange(amps_out)

    start, own = pl.pallas_call(
        between_kernel,
        grid=(pair_dev // block,),
        out_shape=(by_rows, shape(amps_in.shape, f32)),
        in_specs=[SMEM, line, wide, slab, slab, slab, slab, tall, tall],
        out_specs=(tall, slab),
        compiler_params=params(*[shape((2 * block,) + dims, f32) for dims in ((width, 3 * width), (rows, 6 * width))]),
        cost_estimate=pl.CostEstimate(
            flops=6 * pair_dev * width * width * rows,
            bytes_accessed=pair_dev * width * width * 10,
            transcendentals=0,
        ),
        name="between",
    )(place, energy, virt_fock, kept, half, before, sums, start, total)

    to_sum, mine = coupled(amps_far, start, False)
    got = lax.all_to_all(to_sum, "aux", split_axis=0, concat_axis=0, tiled=True)

    return pl.pallas_call(
        last_update_kernel,
        out_shape=shape(amps_in.shape, f32),
        in_specs=[SMEM] + [VMEM] * 5,
        out_specs=VMEM,
        compiler_params=params(got, mine, own, scale, kept, amps_in),
        name="last_update",
    )(place, got, mine, own, scale, kept)


def solution(mesh):
    return jax.shard_map(
        per_device,
        mesh=mesh,
        in_specs=(
            P("pairs", None),
            P("pairs"),
            P("pairs", "aux"),
            P("pairs", "aux"),
            P("pairs", "aux"),
            P(),
            P("pairs", None, "aux"),
            P("pairs", None, "aux"),
            P("pairs", None, None),
            P("pairs", None, None),
            P("pairs", "aux", None),
        ),
        out_specs=P("pairs", "aux", None),
        check_vma=False,
    )
```

time: 274 us -> 262 us (0.956)
  local copies, waits for them, and re-layouts: 21.1 us -> 13.7 us
  other arithmetic: 12.7 us -> 9.23 us
  Pallas kernels: 55.7 us -> 52.8 us
    ppermute x7, waiting for transfers between devices: 25.3 us -> 31.6 us  [per_device(): lax.ppermute(coef_out[turn], 'pairs', [(dev, dev ^ turn + 1) for dev in r...]
    pallas_call x5 -> x7, Pallas kernels: 45.3 us -> 40.3 us  [the longest x1 12.5 us: per_device(): pl.pallas_call(prepare_kernel, grid=(pair_dev // block,), out_shape=(by_r...]
    ppermute x3, waiting for transfers between devices: 3.9 us -> 0.51 us  [per_device(): lax.ppermute(tables, 'aux', [(dev, (dev + turn) % aux_count) for dev in r...]
    unnamed x60 -> x77, local copies, waits for them, and re-layouts: 14.5 us -> 11.7 us
    convert_element_type x2 -> x1, other arithmetic: 6.4 us -> 4.16 us  [per_device(): to_sum = (total * shrink).astype(jnp.float16)]
  transfers between devices with their start and end apart: 13 -> 13, of which waited for: 8 -> 8; matrix products, arithmetic and copies ran while one was open for 3% -> 1% of each run, Pallas kernels for 9% -> 12%
where the time goes in v2:
time: 262 us; the launch traced here: 261 us
  waiting for transfers between devices  105 us (40%)
  blocking collectives  55.2 us (21%)
  Pallas kernels  52.8 us (20%)
  starting transfers between devices  24.5 us (9%)
  local copies, waits for them, and re-layouts  13.7 us (5%)
  other arithmetic  9.23 us (4%)
    all_to_all x1, blocking collectives, per_device(): got = lax.all_to_all(to_sum, 'aux', split_axis=0, concat_axis=0, tiled=True)  55.2 us
    all_to_all x1, waiting for transfers between devices, per_device(): got = lax.all_to_all(to_sum, 'aux', split_axis=0, concat_axis=0, tiled=True)  50.3 us
    ppermute x7, waiting for transfers between devices, per_device(): lax.ppermute(coef_out[turn], 'pairs', [(dev, dev ^ turn + 1) for dev in r...  31.6 us
    all_to_all x2, waiting for transfers between devices, exchange(): lax.all_to_all(packed, ('pairs', 'aux'), split_axis=0, concat_axis=0, til...  22.5 us
    pallas_call x1, Pallas kernels, per_device(): pl.pallas_call(prepare_kernel, grid=(pair_dev // block,), out_shape=(by_r...  12.5 us
    pallas_call x2, Pallas kernels, coupled(): pl.pallas_call(functools.partial(coupling_kernel, groups, scaled), out_sh...  12 us
    unnamed x77, local copies, waits for them, and re-layouts  11.7 us
    pallas_call x1, Pallas kernels, per_device(): pl.pallas_call(between_kernel, grid=(pair_dev // block,), out_shape=(by_r...  9.14 us
  transfers between devices with their start and end apart: 13, of which 8 were waited for; matrix products, arithmetic and copies ran while one was open for 1% of the time, Pallas kernels for 12%

profile of v2, /device:TPU:0, one launch (start us, length us, event | category | flops | bytes accessed | tf_op | source)
XLA Modules:
  0.0 260.7 jit_solution(15702724117190425696)
XLA Ops:
  0.0 0.7 iota_add_fusion
  0.7 0.2 fusion.8
  0.9 0.3 fusion.7
  1.2 0.1 copy.38
  1.3 0.1 reshape.183
  1.5 5.2 %pack_coef.1 = (bf16[6,256,128]{2,1,0:T(8,128)(2,1)S(1)}, bf16[6,256,128]{2,1,0:T(8,128)(2,1)}, bf16[6,256,128]{2,1,0:T(8,128)(2,1)}, bf16[6,256,128]{2,1,0:T(8,...) custom-call(s32[2]{0:T(128)S(1)} %pad_add_fusion.4.place_ref, ...), custom_call_target="tpu_custom_call" | custom-call | tf_op jit(solution)/shard_map/pack_coef/pallas_call | solution.py:387
  6.8 5.1 %collective-permute-start = (s32[64,3]{0,1:T(4,128)S(1)}, s32[64,3]{0,1:T(4,128)S(1)}, u32[]{:S(2)}, u32[]{:S(2)}) collective-permute-start(s32[64,3]{0,1:T(4,128)S(1)} %copy-done.33), channel_id=1, source_target_pairs={{0,3},{1,0},{2,1},{3,2},{4,7},{5,4},{6,5},{7,6},{8,11},{9,8},{10,9... | collective-permute-start | bytes 2312 | tf_op jit(solution)/shard_map/ppermute | solution.py:412
  11.9 1.1 collective-permute-start.2
  13.0 0.9 collective-permute-start.3
  14.1 0.1 broadcast_in_dim.176
  14.2 0.1 broadcast_in_dim.171
  14.4 0.1 broadcast_in_dim.166
  14.6 1.2 collective-permute-start.5
  15.8 0.5 collective-permute-done.1
  16.3 1.0 collective-permute-start.6
  17.4 0.3 fusion.5
  17.7 0.3 fusion.4
  18.2 0.1 copy.41
  18.4 0.1 reshape.184
  18.6 2.0 mask_and_pack.1
  20.6 0.8 copy-done.13
  21.4 3.8 %collective-permute-done.3.rest_0_ = bf16[6,256,128]{2,1,0:T(8,128)(2,1)S(1)} collective-permute-done((bf16[6,256,128]{2,1,0:T(8,128)(2,1)}, bf16[6,256,128]{2,1,0:T(8,128)(2,1)S(1)}, u32[]{:S(2)}, u32[]{:S(2)}) %collective-permute-start.3) | collective-permute-done | bytes 393248 | tf_op jit(solution)/shard_map/ppermute | solution.py:407
  25.3 4.8 %collective-permute-done.4.rest_1_ = bf16[6,256,128]{2,1,0:T(8,128)(2,1)S(1)} collective-permute-done((bf16[6,256,128]{2,1,0:T(8,128)(2,1)}, bf16[6,256,128]{2,1,0:T(8,128)(2,1)S(1)}, u32[]{:S(2)}, u32[]{:S(2)}) %collective-permute-start.4) | collective-permute-done | bytes 393248 | tf_op jit(solution)/shard_map/ppermute | solution.py:407
  30.1 5.3 %collective-permute-done.6.rest_3_ = bf16[6,256,128]{2,1,0:T(8,128)(2,1)} collective-permute-done((bf16[6,256,128]{2,1,0:T(8,128)(2,1)}, bf16[6,256,128]{2,1,0:T(8,128)(2,1)}, u32[]{:S(2)}, u32[]{:S(2)}) %collective-permute-start.6) | collective-permute-done | bytes 393248 | tf_op jit(solution)/shard_map/ppermute | solution.py:407
  35.4 4.7 %all-to-all-start = ((bf16[32,6,32,128]{3,2,1,0:T(8,128)(2,1)}), bf16[32,6,32,128]{3,2,1,0:T(8,128)(2,1)}, u32[]{:S(2)}, u32[]{:S(2)}) async-start(bf16[32,6,32,128]{3,2,1,0:T(8,128)(2,1)} %bitcast.8), calls=%async_computation | async-start | bytes 3145728 | tf_op jit(solution)/shard_map/all_to_all | solution.py:443
  40.1 0.3 collective-permute-start.7
  40.3 2.6 collective-permute-start.8
  42.9 0.1 copy.34
  43.0 0.1 reshape.179
  43.1 0.1 copy.37
  43.2 0.1 reshape.182
  43.4 0.1 copy.36
  43.5 0.1 reshape.181
  43.6 0.1 copy.35
  43.7 0.1 reshape.180
  43.9 3.5 %own_coef.1.own_ref = bf16[42,128,256]{2,1,0:T(8,128)(2,1)S(1)} custom-call(s32[2]{0:T(128)S(1)} %pad_add_fusion.4.place_ref, s32[48]{0:T(128)S(1)} %compare_select_fusion.7.read_ref, bf16[64,256,128]{2,1,0:T(8,128)(2,1)} %coef_ref.3), custom_call_target="tpu_custom_call" | custom-call | tf_op jit(solution)/shard_map/own_coef/pallas_call | solution.py:475
  47.5 12.5 %integrals.1 = (f32[4,64,32,128]{3,2,1,0:T(8,128)}, f32[64,32,128]{2,1,0:T(8,128)S(1)}, f32[64,32,128]{2,1,0:T(8,128)S(1)}, f32[64,1,128]{2,1,0:T(1,128)S(1)}) custom-call(s32[2]{0:T(128)S(1)} %pad_add_fusion.4.place_ref, s32[64]{0:T(128)S(1)} %copy-done.29, s32[512]{0:T(512)S(1)} %pad_add_fusion.3.orbit_ref, f32[256,256]{1,0:T(8,128)S(1)} %copy-done.11, ...), custom_call_target="tpu_custom_call" | custom-call | tf_op jit(solution)/shard_map/integrals/pallas_call | solution.py:458
  60.1 1.8 projectors.2.early_ref
  62.0 7.0 %collective-permute-done.8.rest_1_ = bf16[6,256,128]{2,1,0:T(8,128)(2,1)} collective-permute-done((bf16[6,256,128]{2,1,0:T(8,128)(2,1)}, bf16[6,256,128]{2,1,0:T(8,128)(2,1)}, u32[]{:S(2)}, u32[]{:S(2)}) %collective-permute-start.8) | collective-permute-done | bytes 393248 | tf_op jit(solution)/shard_map/ppermute | solution.py:407
  68.9 10.6 %collective-permute-done.9.rest_2_ = bf16[6,256,128]{2,1,0:T(8,128)(2,1)} collective-permute-done((bf16[6,256,128]{2,1,0:T(8,128)(2,1)}, bf16[6,256,128]{2,1,0:T(8,128)(2,1)}, u32[]{:S(2)}, u32[]{:S(2)}) %collective-permute-start.9) | collective-permute-done | bytes 393248 | tf_op jit(solution)/shard_map/ppermute | solution.py:407
  79.6 1.3 projectors.3.late_ref
  80.9 6.6 %coupling.2 = (f32[4,65,32,128]{3,2,1,0:T(8,128)}, f32[1,128]{1,0:T(1,128)S(1)}) custom-call(s32[2]{0:T(128)S(1)} %pad_add_fusion.4.place_ref, s32[48]{0:T(128)S(1)} %compare_select_fusion.7.read_ref, s32[512]{0:T(512)S(1)} %pad_add_fusion.3.orbit_ref, f32[256,256]{1,0:T(8,128)S(1)} %copy-done.11, bf16[24,128,128]{2,1,0:T(8,128)(2,1)S(1)} %projectors.2.early_ref, ...), custom_call_target="tpu_custom_call" | custom-call | tf_op jit(solution)/shard_map/coupling/pallas_call | solution.py:506
  87.5 4.2 %multiply_convert_fusion = f16[4,65,32,128]{3,2,1,0:T(8,128)(2,1)} fusion(f32[4,65,32,128]{3,2,1,0:T(8,128)} %get-tuple-element.65.old_ref, f32[128]{0:T(128)S(1)} %bitcast.60), kind=kLoop, calls=%fused_computation | loop fusion | flops 2129920 | bytes 6390272 | tf_op jit(solution)/shard_map/convert_element_type | solution.py:522
  91.7 4.8 %all-to-all-start.1 = ((f16[4,65,32,128]{3,2,1,0:T(8,128)(2,1)}), f16[4,65,32,128]{3,2,1,0:T(8,128)(2,1)}, u32[]{:S(2)}, u32[]{:S(2)}) async-start(f16[4,65,32,128]{3,2,1,0:T(8,128)(2,1)} %multiply_convert_fusion), calls=%async_computation.1 | async-start | bytes 4259840 | tf_op jit(solution)/shard_map/all_to_all | solution.py:523
  96.4 50.3 %all-to-all-done.1 = f16[4,65,32,128]{3,2,1,0:T(8,128)(2,1)} async-done(((f16[4,65,32,128]{3,2,1,0:T(8,128)(2,1)}), f16[4,65,32,128]{3,2,1,0:T(8,128)(2,1)}, u32[]{:S(2)}, u32[]{:S(2)}) %all-to-all-start.1) | async-done | bytes 2129952 | tf_op jit(solution)/shard_map/all_to_all | solution.py:523
  146.7 0.8 broadcast_select_fusion
  147.5 2.3 fusion.3.sum_ref
  149.8 1.2 copy-done.6
  151.0 1.2 copy-done.17
  152.2 2.1 first_update.1
  154.4 1.0 copy-done.8
  155.3 0.8 copy-done.21
  156.2 2.9 %all-to-all-start.2 = ((bf16[32,6,32,128]{3,2,1,0:T(8,128)(2,1)}), bf16[32,6,32,128]{3,2,1,0:T(8,128)(2,1)S(1)}, u32[]{:S(2)}, u32[]{:S(2)}) async-start(bf16[32,6,32,128]{3,2,1,0:T(8,128)(2,1)} %bitcast.61), calls=%async_computation.2 | async-start | bytes 3145728 | tf_op jit(solution)/shard_map/all_to_all | solution.py:443
  159.1 1.2 copy-done.9
  160.3 1.0 copy-done.15
  161.3 1.0 copy-done.22
  162.4 9.1 %between.1 = (f32[4,64,32,128]{3,2,1,0:T(8,128)}, f32[64,32,128]{2,1,0:T(8,128)S(1)}) custom-call(s32[2]{0:T(128)S(1)} %pad_add_fusion.4.place_ref, f32[64,1,128]{2,1,0:T(1,128)S(1)} %get-tuple-element.70.energy_ref, bf16[64,128,128]{2,1,0:T(8,128)(2,1)} %fock_ref.3, f32[64,32,128]{2,1,0:T(8,128)S(1)} %copy-done.9, bf16[64,32,128]{2,1,0:T(8,128)(2,1)S(1)} %copy-done.22, ...), custom_call_target="tpu_custom_call" | custom-call | flops 201326592 | bytes 10485760 | tf_op jit(solution)/shard_map/between/pallas_call | solution.py:547
  171.5 1.0 copy-done.19
  172.5 22.5 %all-to-all-done.2 = bf16[32,6,32,128]{3,2,1,0:T(8,128)(2,1)S(1)} async-done(((bf16[32,6,32,128]{3,2,1,0:T(8,128)(2,1)}), bf16[32,6,32,128]{3,2,1,0:T(8,128)(2,1)S(1)}, u32[]{:S(2)}, u32[]{:S(2)}) %all-to-all-start.2) | async-done | bytes 1572896 | tf_op jit(solution)/shard_map/all_to_all | solution.py:443
  195.0 1.1 copy-done.2
  196.1 0.9 copy-done.12
  197.0 5.4 %coupling.3 = (bf16[4,64,32,128]{3,2,1,0:T(8,128)(2,1)}, f32[64,32,128]{2,1,0:T(8,128)S(1)}) custom-call(s32[2]{0:T(128)S(1)} %pad_add_fusion.4.place_ref, s32[48]{0:T(128)S(1)} %compare_select_fusion.7.read_ref, s32[512]{0:T(512)S(1)} %pad_add_fusion.3.orbit_ref, f32[256,256]{1,0:T(8,128)S(1)} %copy-done.12, bf16[24,128,128]{2,1,0:T(8,128)(2,1)S(1)} %projectors.2.early_ref, ...), custom_call_target="tpu_custom_call" | custom-call | tf_op jit(solution)/shard_map/coupling/pallas_call | solution.py:506
  202.5 55.2 %all_to_all.20.got_ref = bf16[4,64,32,128]{3,2,1,0:T(8,128)(2,1)} all-to-all(bf16[4,64,32,128]{3,2,1,0:T(8,128)(2,1)} %get-tuple-element.74), channel_id=1, replica_groups=mesh['pairs'=8,'aux'=4] {'aux'}, dimensions={0} | all-to-all | bytes 4194304 | tf_op jit(solution)/shard_map/all_to_all | solution.py:563
  257.6 3.1 %last_update.1 = f32[64,32,128]{2,1,0:T(8,128)} custom-call(s32[2]{0:T(128)S(1)} %pad_add_fusion.4.place_ref, bf16[4,64,32,128]{3,2,1,0:T(8,128)(2,1)} %all_to_all.20.got_ref, f32[64,32,128]{2,1,0:T(8,128)S(1)} %get-tuple-element.75.mine_ref, f32[64,32,128]{2,1,0:T(8,128)S(1)} %copy-done.20, f32[64,32,128]{2,1,0:T(8,128)S(1)} %copy-done.7, ...), custom_call_target="tpu_custom_call" | custom-call | tf_op jit(solution)/shard_map/last_update/pallas_call | solution.py:565
  (101 shorter events, 1.1 us)
Async XLA Ops:
  1.1 5.6 %copy-start.33 = (s32[64,3]{0,1:T(4,128)S(1)}, s32[64,3]{0,1:T(4,128)}, u32[]{:S(2)}) copy-start(s32[64,3]{0,1:T(4,128)} %param.13) | copy-start | bytes 2308
  1.5 17.1 %copy-start.18 = (f32[64,32,128]{2,1,0:T(8,128)S(1)}, f32[64,32,128]{2,1,0:T(8,128)}, u32[]{:S(2)}) copy-start(f32[64,32,128]{2,1,0:T(8,128)} %amps_ref.1) | copy-start | bytes 3145732
  1.5 17.1 %copy-start.29 = (s32[64]{0:T(128)S(1)}, s32[64]{0:T(128)}, u32[]{:S(2)}) copy-start(s32[64]{0:T(128)} %count_ref.3) | copy-start | bytes 772
  6.7 5.1 %copy-start.30 = (bf16[6,256,128]{2,1,0:T(8,128)(2,1)}, bf16[6,256,128]{2,1,0:T(8,128)(2,1)S(1)}, u32[]{:S(2)}) copy-start(bf16[6,256,128]{2,1,0:T(8,128)(2,1)S(1)} %get-tuple-element.60) | copy-start | bytes 1179652
  6.7 6.3 %copy-start.31 = (bf16[6,256,128]{2,1,0:T(8,128)(2,1)}, bf16[6,256,128]{2,1,0:T(8,128)(2,1)S(1)}, u32[]{:S(2)}) copy-start(bf16[6,256,128]{2,1,0:T(8,128)(2,1)S(1)} %get-tuple-element.59) | copy-start | bytes 1179652
  6.7 7.2 %copy-start.32 = (bf16[6,256,128]{2,1,0:T(8,128)(2,1)}, bf16[6,256,128]{2,1,0:T(8,128)(2,1)S(1)}, u32[]{:S(2)}) copy-start(bf16[6,256,128]{2,1,0:T(8,128)(2,1)S(1)} %get-tuple-element.58) | copy-start | bytes 1179652
  6.8 7.9 %collective-permute-start = (s32[64,3]{0,1:T(4,128)S(1)}, s32[64,3]{0,1:T(4,128)S(1)}, u32[]{:S(2)}, u32[]{:S(2)}) collective-permute-start(s32[64,3]{0,1:T(4,128)S(1)} %copy-done.33), channel_id=1, source_target_pairs={{0,3},{1,0},{2,1},{3,2},{4,7},{5,4},{6,5},{7,6},{8,11},{9,8},{10,9... | collective-permute-start | bytes 2312 | tf_op jit(solution)/shard_map/ppermute | solution.py:412
  11.8 4.5 %collective-permute-start.1 = (s32[64,3]{0,1:T(4,128)S(1)}, s32[64,3]{0,1:T(4,128)S(1)}, u32[]{:S(2)}, u32[]{:S(2)}) collective-permute-start(s32[64,3]{0,1:T(4,128)S(1)} %copy-done.33), channel_id=1, source_target_pairs={{0,2},{1,3},{2,0},{3,1},{4,6},{5,7},{6,4},{7,5},{8,10},{9,11},{10,... | collective-permute-start | bytes 2312 | tf_op jit(solution)/shard_map/ppermute | solution.py:412
  11.9 5.5 %collective-permute-start.2 = (s32[64,3]{0,1:T(4,128)S(1)}, s32[64,3]{0,1:T(4,128)S(1)}, u32[]{:S(2)}, u32[]{:S(2)}) collective-permute-start(s32[64,3]{0,1:T(4,128)S(1)} %copy-done.33), channel_id=1, source_target_pairs={{0,1},{1,2},{2,3},{3,0},{4,5},{5,6},{6,7},{7,4},{8,9},{9,10},{10,1... | collective-permute-start | bytes 2312 | tf_op jit(solution)/shard_map/ppermute | solution.py:412
  13.0 12.3 %collective-permute-start.3 = (bf16[6,256,128]{2,1,0:T(8,128)(2,1)}, bf16[6,256,128]{2,1,0:T(8,128)(2,1)S(1)}, u32[]{:S(2)}, u32[]{:S(2)}) collective-permute-start(bf16[6,256,128]{2,1,0:T(8,128)(2,1)} %get-tuple-element.50), channel_id=1, source_target_pairs={{0,8},{4,12},{8,0},{12,4},{16,24},{20,28},{24,16},{28,20},{1,9},{5... | collective-permute-start | bytes 1179656 | tf_op jit(solution)/shard_map/ppermute | solution.py:407
  13.9 16.2 %collective-permute-start.4 = (bf16[6,256,128]{2,1,0:T(8,128)(2,1)}, bf16[6,256,128]{2,1,0:T(8,128)(2,1)S(1)}, u32[]{:S(2)}, u32[]{:S(2)}) collective-permute-start(bf16[6,256,128]{2,1,0:T(8,128)(2,1)} %get-tuple-element.51), channel_id=1, source_target_pairs={{0,12},{4,8},{8,4},{12,0},{16,28},{20,24},{24,20},{28,16},{1,13},{... | collective-permute-start | bytes 1179656 | tf_op jit(solution)/shard_map/ppermute | solution.py:407
  14.6 15.4 %collective-permute-start.5 = (bf16[6,256,128]{2,1,0:T(8,128)(2,1)}, bf16[6,256,128]{2,1,0:T(8,128)(2,1)S(1)}, u32[]{:S(2)}, u32[]{:S(2)}) collective-permute-start(bf16[6,256,128]{2,1,0:T(8,128)(2,1)} %get-tuple-element.52), channel_id=1, source_target_pairs={{0,16},{4,20},{8,24},{12,28},{16,0},{20,4},{24,8},{28,12},{1,17},{... | collective-permute-start | bytes 1179656 | tf_op jit(solution)/shard_map/ppermute | solution.py:407
  16.3 19.0 %collective-permute-start.6 = (bf16[6,256,128]{2,1,0:T(8,128)(2,1)}, bf16[6,256,128]{2,1,0:T(8,128)(2,1)}, u32[]{:S(2)}, u32[]{:S(2)}) collective-permute-start(bf16[6,256,128]{2,1,0:T(8,128)(2,1)} %get-tuple-element.53), channel_id=1, source_target_pairs={{0,20},{4,16},{8,28},{12,24},{16,4},{20,0},{24,12},{28,8},{1,21},{... | collective-permute-start | bytes 1179656 | tf_op jit(solution)/shard_map/ppermute | solution.py:407
  18.5 24.6 %copy-start.36 = (s32[64,2]{0,1:T(2,128)S(1)}, s32[64,2]{0,1:T(2,128)}, u32[]{:S(2)}) copy-start(s32[64,2]{0,1:T(2,128)} %param.11) | copy-start | bytes 1540
  18.6 24.8 %copy-start.34 = (s32[64,3]{0,1:T(4,128)S(1)}, s32[64,3]{0,1:T(4,128)}, u32[]{:S(2)}) copy-start(s32[64,3]{0,1:T(4,128)} %param.15) | copy-start | bytes 2308
  18.6 25.0 %copy-start.35 = (s32[64,3]{0,1:T(4,128)S(1)}, s32[64,3]{0,1:T(4,128)}, u32[]{:S(2)}) copy-start(s32[64,3]{0,1:T(4,128)} %param.14) | copy-start | bytes 2308
  20.6 0.8 copy-start.13
  21.4 26.1 %copy-start.3 = (f32[64,32,128]{2,1,0:T(8,128)}, f32[64,32,128]{2,1,0:T(8,128)S(1)}, u32[]{:S(2)}) copy-start(f32[64,32,128]{2,1,0:T(8,128)S(1)} %get-tuple-element.62.kept_ref) | copy-start | bytes 3145732
  25.3 18.6 %copy-start.23 = (bf16[6,256,128]{2,1,0:T(8,128)(2,1)}, bf16[6,256,128]{2,1,0:T(8,128)(2,1)S(1)}, u32[]{:S(2)}) copy-start(bf16[6,256,128]{2,1,0:T(8,128)(2,1)S(1)} %collective-permute-done.3.rest_0_) | copy-start | bytes 1179652
  30.0 13.8 %copy-start.25 = (bf16[6,256,128]{2,1,0:T(8,128)(2,1)}, bf16[6,256,128]{2,1,0:T(8,128)(2,1)S(1)}, u32[]{:S(2)}) copy-start(bf16[6,256,128]{2,1,0:T(8,128)(2,1)S(1)} %collective-permute-done.4.rest_1_) | copy-start | bytes 1179652
  30.1 13.8 %copy-start.27 = (bf16[6,256,128]{2,1,0:T(8,128)(2,1)}, bf16[6,256,128]{2,1,0:T(8,128)(2,1)S(1)}, u32[]{:S(2)}) copy-start(bf16[6,256,128]{2,1,0:T(8,128)(2,1)S(1)} %collective-permute-done.5.rest_2_) | copy-start | bytes 1179652
  35.4 45.5 %all-to-all-start = ((bf16[32,6,32,128]{3,2,1,0:T(8,128)(2,1)}), bf16[32,6,32,128]{3,2,1,0:T(8,128)(2,1)}, u32[]{:S(2)}, u32[]{:S(2)}) async-start(bf16[32,6,32,128]{3,2,1,0:T(8,128)(2,1)} %bitcast.8), calls=%async_computation | async-start | bytes 3145728 | tf_op jit(solution)/shard_map/all_to_all | solution.py:443
  40.1 21.9 %collective-permute-start.7 = (bf16[6,256,128]{2,1,0:T(8,128)(2,1)}, bf16[6,256,128]{2,1,0:T(8,128)(2,1)}, u32[]{:S(2)}, u32[]{:S(2)}) collective-permute-start(bf16[6,256,128]{2,1,0:T(8,128)(2,1)} %copy-done.32), channel_id=1, source_target_pairs={{0,4},{4,0},{8,12},{12,8},{16,20},{20,16},{24,28},{28,24},{1,5},{5... | collective-permute-start | bytes 1179656 | tf_op jit(solution)/shard_map/ppermute | solution.py:407
  40.3 28.6 %collective-permute-start.8 = (bf16[6,256,128]{2,1,0:T(8,128)(2,1)}, bf16[6,256,128]{2,1,0:T(8,128)(2,1)}, u32[]{:S(2)}, u32[]{:S(2)}) collective-permute-start(bf16[6,256,128]{2,1,0:T(8,128)(2,1)} %copy-done.31), channel_id=1, source_target_pairs={{0,24},{4,28},{8,16},{12,20},{16,8},{20,12},{24,0},{28,4},{1,25},{... | collective-permute-start | bytes 1179656 | tf_op jit(solution)/shard_map/ppermute | solution.py:407
  42.9 36.7 %collective-permute-start.9 = (bf16[6,256,128]{2,1,0:T(8,128)(2,1)}, bf16[6,256,128]{2,1,0:T(8,128)(2,1)}, u32[]{:S(2)}, u32[]{:S(2)}) collective-permute-start(bf16[6,256,128]{2,1,0:T(8,128)(2,1)} %copy-done.30), channel_id=1, source_target_pairs={{0,28},{4,24},{8,20},{12,16},{16,12},{20,8},{24,4},{28,0},{1,29},{... | collective-permute-start | bytes 1179656 | tf_op jit(solution)/shard_map/ppermute | solution.py:407
  43.9 3.6 %copy-start = (bf16[64,128,128]{2,1,0:T(8,128)(2,1)S(1)}, bf16[64,128,128]{2,1,0:T(8,128)(2,1)}, u32[]{:S(2)}) copy-start(bf16[64,128,128]{2,1,0:T(8,128)(2,1)} %fock_ref.3) | copy-start | bytes 6291460
  43.9 3.6 %copy-start.11 = (f32[256,256]{1,0:T(8,128)S(1)}, f32[256,256]{1,0:T(8,128)}, u32[]{:S(2)}) copy-start(f32[256,256]{1,0:T(8,128)} %occ_ref.5) | copy-start | bytes 786436
  43.9 3.6 %copy-start.14 = (bf16[64,32,128]{2,1,0:T(8,128)(2,1)S(1)}, bf16[64,32,128]{2,1,0:T(8,128)(2,1)}, u32[]{:S(2)}) copy-start(bf16[64,32,128]{2,1,0:T(8,128)(2,1)} %copy-done.13) | copy-start | bytes 1572868
  47.5 12.6 %copy-start.24 = (bf16[6,256,128]{2,1,0:T(8,128)(2,1)S(1)}, bf16[6,256,128]{2,1,0:T(8,128)(2,1)}, u32[]{:S(2)}) copy-start(bf16[6,256,128]{2,1,0:T(8,128)(2,1)} %copy-done.23) | copy-start | bytes 1179652
  47.5 12.6 %copy-start.26 = (bf16[6,256,128]{2,1,0:T(8,128)(2,1)S(1)}, bf16[6,256,128]{2,1,0:T(8,128)(2,1)}, u32[]{:S(2)}) copy-start(bf16[6,256,128]{2,1,0:T(8,128)(2,1)} %copy-done.25) | copy-start | bytes 1179652
  47.5 12.6 %copy-start.28 = (bf16[6,256,128]{2,1,0:T(8,128)(2,1)S(1)}, bf16[6,256,128]{2,1,0:T(8,128)(2,1)}, u32[]{:S(2)}) copy-start(bf16[6,256,128]{2,1,0:T(8,128)(2,1)} %copy-done.27) | copy-start | bytes 1179652
  60.1 1.8 copy-start.5
  60.1 1.8 copy-start.16
  80.9 6.6 %copy-start.1 = (bf16[18,128,128]{2,1,0:T(8,128)(2,1)}, bf16[18,128,128]{2,1,0:T(8,128)(2,1)S(1)}, u32[]{:S(2)}) copy-start(bf16[18,128,128]{2,1,0:T(8,128)(2,1)S(1)} %projectors.3.late_ref) | copy-start | bytes 1769476
  91.7 55.1 %all-to-all-start.1 = ((f16[4,65,32,128]{3,2,1,0:T(8,128)(2,1)}), f16[4,65,32,128]{3,2,1,0:T(8,128)(2,1)}, u32[]{:S(2)}, u32[]{:S(2)}) async-start(f16[4,65,32,128]{3,2,1,0:T(8,128)(2,1)} %multiply_convert_fusion), calls=%async_computation.1 | async-start | bytes 4259840 | tf_op jit(solution)/shard_map/all_to_all | solution.py:523
  96.4 53.3 %copy-start.4 = (f32[64,32,128]{2,1,0:T(8,128)S(1)}, f32[64,32,128]{2,1,0:T(8,128)}, u32[]{:S(2)}) copy-start(f32[64,32,128]{2,1,0:T(8,128)} %copy-done.3) | copy-start | bytes 3145732
  149.8 1.2 copy-start.6
  151.0 1.2 copy-start.17
  154.4 1.0 copy-start.8
  155.3 0.8 copy-start.21
  156.2 38.8 %all-to-all-start.2 = ((bf16[32,6,32,128]{3,2,1,0:T(8,128)(2,1)}), bf16[32,6,32,128]{3,2,1,0:T(8,128)(2,1)S(1)}, u32[]{:S(2)}, u32[]{:S(2)}) async-start(bf16[32,6,32,128]{3,2,1,0:T(8,128)(2,1)} %bitcast.61), calls=%async_computation.2 | async-start | bytes 3145728 | tf_op jit(solution)/shard_map/all_to_all | solution.py:443
  159.0 1.2 copy-start.9
  160.3 1.0 copy-start.15
  161.3 1.0 copy-start.22
  171.5 1.0 copy-start.19
  195.0 1.1 copy-start.2
  196.0 0.9 copy-start.12
  202.4 55.2 %copy-start.7 = (f32[64,32,128]{2,1,0:T(8,128)S(1)}, f32[64,32,128]{2,1,0:T(8,128)}, u32[]{:S(2)}) copy-start(f32[64,32,128]{2,1,0:T(8,128)} %copy-done.5) | copy-start | bytes 3145732
  202.4 55.2 %copy-start.10 = (f32[64,32,128]{2,1,0:T(8,128)S(1)}, f32[64,32,128]{2,1,0:T(8,128)}, u32[]{:S(2)}) copy-start(f32[64,32,128]{2,1,0:T(8,128)} %copy-done.8) | copy-start | bytes 3145732
  202.5 55.2 %copy-start.20 = (f32[64,32,128]{2,1,0:T(8,128)S(1)}, f32[64,32,128]{2,1,0:T(8,128)}, u32[]{:S(2)}) copy-start(f32[64,32,128]{2,1,0:T(8,128)} %copy-done.19) | copy-start | bytes 3145732
